TPU v7x, 256 devices: a whole 4x4x8 slice. The times are simulated.
256 devices in a mesh: dir: 8 (over z_hi, core), dom: 32 (over y, z_lo, x).
Axes of the slice: x: 4, y: 4, z: 8 (z_hi: 4, z_lo: 2; z = z_hi * 2 + z_lo), core: 2. Of those that a mesh axis runs over, the one named last changes fastest.
Arguments:
- images: bfloat16 [8192, 4096], P('dom'), may hold values from -12 to 12
- refs: bfloat16 [2048, 4096], P(('dir', 'dom')), may hold values from -0.8 to 0.8
- ctf: float32 [64, 2048], replicated, may hold values from -1 to 1
- noise_var: float32 [2048], replicated, may hold values from 0.5 to 2
- shifts: int32 [8192, 2], P('dom'), may hold values from -4 to 4
- ctf_class: int32 [8192], P('dom'), may hold values from 0 to 63
- psi_prev: int32 [8192], P('dom'), may hold values from 0 to 15
- earlier_direction_range: int32 [8192], P('dom'), may hold values from 0 to 7
- view_range: int32 [128], P('dir'), may hold values from 0 to 7
Outputs:
- class_sums: float32 [2048, 4096], P(('dir', 'dom'))
- weight_sums: float32 [2048, 2048], P(('dir', 'dom'))
- log_norm: float32 [8192], P('dom')
- peak_prob: float32 [8192], P('dom')
All inputs are finite; a program needn't handle non-finite values.
Results may differ from a plain program's by a relative error of at most 0.0095.
The roundings to bfloat16 on the way count: a program that leaves them out, or rounds other values in their place, can miss the bound.
Values may be sent and summed in bfloat16 or wider, within the bound.
A program may use at most 64 MiB of HBM per device.

v0:
```python
import math

import jax
import jax.numpy as jnp
from jax import lax
from jax.sharding import PartitionSpec as P

CROP = 64
HALF = 32
OFFSETS = 9
PSI_STEPS = 16
CTF_GROUPS = 64


range_reward = 1.5
inplane_angle_width = 3.0


def phase_angles(shift_y, shift_x):
    pixels = jnp.arange(CROP * HALF, dtype=jnp.int32)
    freq_y = pixels // HALF
    freq_x = pixels % HALF
    index = (freq_y * shift_y[..., None] + freq_x * shift_x[..., None]) % CROP
    return index.astype(jnp.float32) * (2.0 * math.pi / CROP)


def offset_tables():
    offsets = jnp.arange(OFFSETS, dtype=jnp.int32)
    angles = phase_angles(offsets // 3 - 1, offsets % 3 - 1)
    return (jnp.cos(angles), jnp.sin(angles))


def align_images(images, shifts, ctf_class, ctf, noise_var):
    angles = phase_angles(shifts[:, 0], shifts[:, 1])
    cosine_part = jnp.cos(angles)
    sine_part = jnp.sin(angles)
    pixels = CROP * HALF
    real_part = images[:, :pixels].astype(jnp.float32)
    imag_part = images[:, pixels:].astype(jnp.float32)
    weighting = jnp.take(ctf, ctf_class, axis=0) / noise_var[None, :]
    aligned_real = (real_part * cosine_part + imag_part * sine_part) * weighting
    aligned_imag = (imag_part * cosine_part - real_part * sine_part) * weighting
    return jnp.concatenate([aligned_real, aligned_imag], axis=1).astype(jnp.bfloat16)


def shift_block(ref_rows, cosine_row, sine_row):
    pixels = CROP * HALF
    real_part = ref_rows[:, :pixels].astype(jnp.float32)
    imag_part = ref_rows[:, pixels:].astype(jnp.float32)
    shifted_real = real_part * cosine_row[None, :] - imag_part * sine_row[None, :]
    shifted_imag = real_part * sine_row[None, :] + imag_part * cosine_row[None, :]
    return jnp.concatenate([shifted_real, shifted_imag], axis=1).astype(jnp.bfloat16)


def ref_energy(ref_rows, gain_table):
    pixels = CROP * HALF
    real_part = ref_rows[:, :pixels].astype(jnp.float32)
    imag_part = ref_rows[:, pixels:].astype(jnp.float32)
    magnitude = real_part * real_part + imag_part * imag_part
    return lax.dot_general(
        gain_table,
        magnitude,
        (((1,), (1,)), ((), ())),
        precision=lax.Precision.HIGHEST,
        preferred_element_type=jnp.float32,
    )


def prior_terms(row_index, psi_prev, earlier_direction_range, view_table):
    psi_rows = row_index % PSI_STEPS
    angular_separation = jnp.abs(psi_rows[None, :] - psi_prev[:, None])
    angular_separation = jnp.minimum(angular_separation, PSI_STEPS - angular_separation).astype(
        jnp.float32
    )
    views = row_index // PSI_STEPS
    view_ids = jnp.arange(view_table.shape[0], dtype=jnp.int32)
    row_span = jnp.sum(
        jnp.where(views[:, None] == view_ids[None, :], view_table[None, :], 0), axis=1
    )
    prior_reward = jnp.where(
        row_span[None, :] == earlier_direction_range[:, None],
        jnp.float32(range_reward),
        jnp.float32(0.0),
    )
    return prior_reward - angular_separation * angular_separation * jnp.float32(
        0.5 / (inplane_angle_width * inplane_angle_width)
    )


def combine_scores(cross, energy, ctf_class, prior):
    penalty = 0.5 * jnp.take(energy, ctf_class, axis=0)
    return cross - penalty[None, :, :] + prior[None, :, :]


def insert_images(posterior, aligned, offset_cos, offset_sin):
    pixels = CROP * HALF

    def add_offset(offset, total):
        weights_now = posterior[offset]
        summed = lax.dot_general(
            weights_now, aligned, (((0,), (0,)), ((), ())), preferred_element_type=jnp.float32
        )
        cosine_row = offset_cos[offset][None, :]
        sine_row = offset_sin[offset][None, :]
        summed_real = summed[:, :pixels]
        imaginary_total = summed[:, pixels:]
        turned = jnp.concatenate(
            [
                summed_real * cosine_row + imaginary_total * sine_row,
                imaginary_total * cosine_row - summed_real * sine_row,
            ],
            axis=1,
        )
        return total + turned

    initial = jnp.zeros((posterior.shape[2], 2 * pixels), jnp.float32)
    return lax.fori_loop(0, OFFSETS, add_offset, initial)


def class_mass(posterior, ctf_class):
    particle_mass = jnp.sum(posterior.astype(jnp.float32), axis=0)
    onehot_table = (ctf_class[:, None] == jnp.arange(CTF_GROUPS, dtype=jnp.int32)[None, :]).astype(
        jnp.float32
    )
    return lax.dot_general(
        particle_mass,
        onehot_table,
        (((0,), (0,)), ((), ())),
        precision=lax.Precision.HIGHEST,
        preferred_element_type=jnp.float32,
    )


def per_device(
    images, refs, ctf, noise_var, shifts, ctf_class, psi_prev, earlier_direction_range, view_range
):
    aligned = align_images(images, shifts, ctf_class, ctf, noise_var)
    offset_cos, offset_sin = offset_tables()
    gain_table = ctf * ctf / noise_var[None, :]
    piece = lax.all_gather(refs, "dom", axis=0, tiled=True)
    row_index = jnp.arange(piece.shape[0], dtype=jnp.int32)
    energy = ref_energy(piece, gain_table)

    def one_offset(tables):
        shifted = shift_block(piece, tables[0], tables[1])
        return lax.dot_general(
            aligned, shifted, (((1,), (1,)), ((), ())), preferred_element_type=jnp.float32
        )

    cross = lax.map(one_offset, (offset_cos, offset_sin))
    scores = combine_scores(
        cross,
        energy,
        ctf_class,
        prior_terms(row_index, psi_prev, earlier_direction_range, view_range),
    )
    top = lax.pmax(jnp.max(scores, axis=(0, 2)), "dir")
    total = lax.psum(jnp.sum(jnp.exp(scores - top[None, :, None]), axis=(0, 2)), "dir")
    log_norm = top + jnp.log(total)
    peak_prob = jnp.exp(top - log_norm)
    posterior = jnp.exp(scores - log_norm[None, :, None]).astype(jnp.bfloat16)
    class_sums = lax.psum_scatter(
        insert_images(posterior, aligned, offset_cos, offset_sin),
        "dom",
        scatter_dimension=0,
        tiled=True,
    )
    masses = class_mass(posterior, ctf_class)
    owned_mass = lax.psum_scatter(masses, "dom", scatter_dimension=0, tiled=True)
    weight_sums = jnp.dot(owned_mass, gain_table, precision=lax.Precision.HIGHEST)
    return (class_sums, weight_sums, log_norm, peak_prob)


def solution(mesh):
    placed = (
        P("dom", None),
        P(("dir", "dom"), None),
        P(),
        P(),
        P("dom", None),
        P("dom"),
        P("dom"),
        P("dom"),
        P("dir"),
    )
    return jax.shard_map(
        per_device,
        mesh=mesh,
        in_specs=placed,
        out_specs=(P(("dir", "dom"), None), P(("dir", "dom"), None), P("dom"), P("dom")),
        check_vma=False,
    )
```

profile of v0, /device:TPU:2, one launch (start us, length us, event | category | flops | bytes accessed | tf_op | source)
XLA Modules:
  0.0 710.8 jit_solution(5796960012372682684)
XLA Ops:
  8.7 3.5 gather_fusion
  12.9 1.3 fusion.45
  14.2 11.1 %fusion.18 = (bf16[256,2048]{1,0:T(8,128)(2,1)S(1)}, bf16[256,2048]{1,0:T(8,128)(2,1)S(1)}) fusion(s32[256]{0:T(256)S(1)} %bitcast.38, s32[2048]{0:T(1024)S(1)} %get-tuple-element.210, s32[256]{0:T(256)S(1)} %bitcast.37, s32[2048]{0:T(1024)S(1)} %get-tuple-element.211, bf16[256,4096]{1,0:T(8,128)(2,1)} %param.13, f32[2048]{0:T(1024)S(1)} %copy-done.3, ...), kind=kLoop, calls=%fused_computation.41 | loop fusion | flops 15728640 | bytes 6318336 | tf_op jit(solution)/shard_map/convert.2
  25.5 142.6 %all-gather.2.cloned.1.call-done = bf16[256,4096]{1,0:T(8,128)(2,1)} async-done(((bf16[8,4096]{1,0:T(8,128)(2,1)}), bf16[256,4096]{1,0:T(8,128)(2,1)}) %all-gather.2.cloned.1.call-update) | async-done | bytes 2097168 | tf_op jit(solution)/shard_map/all_gather | solution.py:140
  168.1 3.6 fusion.25
  171.7 1.0 gather_fusion.1
  172.7 42.3 %while.24 = (s32[]{:T(128)}, f32[9,256,256]{2,1,0:T(8,128)}, bf16[256,4096]{1,0:T(8,128)(2,1)}, f32[9,2048]{1,0:T(8,128)}, f32[9,2048]{1,0:T(8,128)S(1)}, /*index=5*/bf16[256,4096]{1,0:T(8,128)(2,1)S(1)}, s32[]{:T(128)}) while((s32[]{:T(128)}, f32[9,256,256]{2,1,0:T(8,128)}, bf16[256,4096]{1,0:T(8,128)(2,1)}, f32[9,2048]{1,0:T(8,128)}, ...), condition=%wide.region_1.2_spmd, body=%wide.region_0.1_spmd.sunk | while | flops 546308096 | bytes 9748573 | solution.py:150
  172.7 0.9 constant_dynamic-slice_fusion.6
  173.5 2.2 fusion.74
  178.2 2.2 fusion.74
  182.9 2.2 fusion.74
  187.6 2.2 fusion.74
  192.3 2.2 fusion.74
  197.0 2.2 fusion.74
  201.7 2.2 fusion.74
  206.4 2.2 fusion.74
  211.1 2.2 fusion.74
  214.9 0.9 fusion.39
  215.9 2.0 fusion.31
  217.9 14.2 %pmax.7 = f32[256]{0:T(256)S(1)} all-reduce(f32[256]{0:T(256)S(1)} %fusion.31), channel_id=1, replica_groups=mesh['dir'=8,'dom'=32] {'dir'}, use_global_device_ids=true, to_apply=%region_4.5 | all-reduce | flops 256 | bytes 2048 | tf_op jit(solution)/shard_map/pmax | solution.py:157
  232.1 2.2 exponential_reduce_fusion
  234.3 15.0 %psum.7 = f32[256]{0:T(256)S(1)} all-reduce(f32[256]{0:T(256)S(1)} %exponential_reduce_fusion), channel_id=1, replica_groups=mesh['dir'=8,'dom'=32] {'dir'}, use_global_device_ids=true, to_apply=%region_6.7 | all-reduce | flops 256 | bytes 2048 | tf_op jit(solution)/shard_map/psum | solution.py:158
  249.9 3.2 convert_reduce_fusion
  253.2 1.1 fusion.44
  254.5 72.5 %while.25 = (s32[]{:T(128)}, f32[256,4096]{1,0:T(8,128)}, bf16[9,256,256]{2,1,0:T(8,128)(2,1)}, bf16[256,4096]{1,0:T(8,128)(2,1)S(1)}, f32[9,2048]{1,0:T(8,128)}...) while((s32[]{:T(128)}, f32[256,4096]{1,0:T(8,128)}, bf16[9,256,256]{2,1,0:T(8,128)(2,1)}, ...), condition=%wide.region_8.9_spmd.clone, body=%wide.region_7.8_spmd.clone.sunk | while | flops 543162368 | bytes 60997796 | solution.py:117
  255.4 1.6 fusion.78
  257.6 1.6 copy-done.1
  259.2 1.4 maximum_add_fusion.2
  260.6 1.9 copy-done.2
  263.4 1.6 fusion.78
  265.7 1.6 copy-done.1
  267.3 1.4 maximum_add_fusion.2
  268.7 1.9 copy-done.2
  271.5 1.6 fusion.78
  273.7 1.6 copy-done.1
  275.3 1.4 maximum_add_fusion.2
  276.7 1.9 copy-done.2
  279.5 1.6 fusion.78
  281.8 1.6 copy-done.1
  283.4 1.4 maximum_add_fusion.2
  284.8 1.9 copy-done.2
  287.6 1.6 fusion.78
  289.8 1.6 copy-done.1
  291.4 1.4 maximum_add_fusion.2
  292.9 1.9 copy-done.2
  295.6 1.6 fusion.78
  297.9 1.6 copy-done.1
  299.5 1.4 maximum_add_fusion.2
  300.9 1.9 copy-done.2
  303.7 1.6 fusion.78
  305.9 1.6 copy-done.1
  307.6 1.4 maximum_add_fusion.2
  309.0 1.9 copy-done.2
  311.8 1.6 fusion.78
  314.0 1.6 copy-done.1
  315.6 1.4 maximum_add_fusion.2
  317.0 1.9 copy-done.2
  319.8 1.6 fusion.78
  322.1 1.6 copy-done.1
  323.7 1.4 maximum_add_fusion.2
  325.1 1.9 copy-done.2
  328.9 207.1 %all-reduce.3.cloned.1.call-done = f32[256,64]{1,0:T(8,128)} async-done(((f32[256,64]{1,0:T(8,128)}), f32[256,64]{1,0:T(8,128)}) %all-reduce.3.cloned.1.call-update) | async-done | bytes 65552
  536.1 1.7 fusion.40
  537.8 166.5 %reduce-scatter.2.cloned.1.call-done = f32[8,4096]{1,0:T(8,128)} async-done(((f32[256,4096]{1,0:T(8,128)}), f32[8,4096]{1,0:T(8,128)}) %reduce-scatter.2.cloned.1.call-update) | async-done | bytes 131088 | tf_op jit(solution)/shard_map/reduce_scatter | solution.py:162
  (107 shorter events, 38.6 us)
Async XLA Ops:
  7.2 160.9 %all-gather.2.cloned.1.call-start = ((), (), s32[]{:S(2)}) async-start(), calls=%async_computation.1 | async-start | bytes 2162688 | tf_op jit(solution)/shard_map/all_gather | solution.py:140
  7.9 528.2 %all-reduce.3.cloned.1.call-start = ((), (), s32[]{:S(2)}) async-start(), calls=%async_computation.3 | async-start | bytes 262144
  8.7 4.1 copy-start.8
  8.7 4.2 copy-start.4
  8.7 4.2 copy-start.6
  8.7 5.5 copy-start.3
  12.9 12.4 %copy-start.7 = (pred[256]{0:T(512)(128)(4,1)}, pred[256]{0:T(512)(128)(4,1)S(1)}, u32[]{:S(2)}) copy-start(pred[256]{0:T(512)(128)(4,1)S(1)} %compare_and_fusion) | copy-start | bytes 772
  25.2 142.8 %copy-start = (f32[64,2048]{1,0:T(8,128)S(1)}, f32[64,2048]{1,0:T(8,128)}, u32[]{:S(2)}) copy-start(f32[64,2048]{1,0:T(8,128)} %param.15) | copy-start | bytes 1572868
  249.9 3.2 copy-start.5
  254.3 450.0 %reduce-scatter.2.cloned.1.call-start = ((), (), s32[]{:S(2)}) async-start(), calls=%async_computation.2 | async-start | bytes 4325376 | tf_op jit(solution)/shard_map/reduce_scatter | solution.py:162
  257.0 2.2 copy-start.1
  260.6 1.9 copy-start.2
  265.1 2.2 copy-start.1
  268.7 1.9 copy-start.2
  273.1 2.2 copy-start.1
  276.7 1.9 copy-start.2
  281.2 2.2 copy-start.1
  284.8 1.9 copy-start.2
  289.2 2.2 copy-start.1
  292.8 1.9 copy-start.2
  297.3 2.2 copy-start.1
  300.9 1.9 copy-start.2
  305.3 2.2 copy-start.1
  309.0 1.9 copy-start.2
  313.4 2.2 copy-start.1
  317.0 1.9 copy-start.2
  321.5 2.2 copy-start.1
  325.1 1.9 copy-start.2
  327.0 0.7 copy-start.9
Sparse Core Ops, SparseCore 0:
  9.8 158.2 all-gather.1
  254.4 281.6 all-reduce.2
  539.4 164.8 reduce-scatter.1
where the time goes:
time: 717 us; the launch traced here: 711 us
  waiting for transfers between devices  517 us (72%)
  other arithmetic  60.8 us (8%)
  local copies, waits for them, and re-layouts  60.6 us (8%)
  blocking collectives  29.2 us (4%)
  matrix products  27.8 us (4%)
  between operations  14.5 us (2%)
    unnamed x4, waiting for transfers between devices  208 us
    reduce_scatter x1, waiting for transfers between devices, per_device(): lax.psum_scatter(insert_images(posterior, aligned, offset_cos, offset_sin...  166 us
    all_gather x1, waiting for transfers between devices, per_device(): piece = lax.all_gather(refs, 'dom', axis=0, tiled=True)  143 us
    while x36, local copies, waits for them, and re-layouts  31.9 us
    another operation x10, other arithmetic  31.1 us
    psum x1, blocking collectives, per_device(): lax.psum(jnp.sum(jnp.exp(scores - top[None, :, None]), axis=(0, 2)), 'dir')  15 us
    dot_general x9, matrix products, add_offset(): lax.dot_general(weights_now, aligned, (((0,), (0,)), ((), ())), preferred...  14.8 us
  transfers between devices with their start and end apart: 3, of which 3 were waited for; matrix products, arithmetic and copies ran while one was open for 8% of the time, Pallas kernels for 0%

commit v1 on v0

v1 whole, which is shorter than its diff:
```python
import math

import jax
import jax.numpy as jnp
import numpy as np
from jax import lax
from jax.experimental import pallas as pl
from jax.experimental.pallas import tpu as pltpu
from jax.sharding import PartitionSpec as P

CROP = 64
HALF = 32
PIX = 2048
OFFSETS = 9
GROUPS = 64
N = 256
BLOCKS = 32
HP = 1024
WIDTHS = (HP + 128, HP)
THETA = 2.0 * math.pi / CROP

F32 = jnp.float32
BF16 = jnp.bfloat16
MESH = pl.DeviceIdType.MESH

PAIRS = ((0, 1), (1, 0), (1, 1), (1, -1))


def offset_index(ty, tx):
    return (ty + 1) * 3 + (tx + 1)


def phase_constants():
    pixels = np.arange(PIX)
    alpha = THETA * (pixels // HALF)
    beta = THETA * (pixels % HALF)
    rows = []
    for ty, tx in PAIRS:
        angle = ty * alpha + tx * beta
        rows += [np.cos(angle), np.sin(angle)]
    ca, sa, cb, sb = np.cos(alpha), np.sin(alpha), np.cos(beta), np.sin(beta)
    rows += [cb, ca, ca * cb, -sa * sb, sb, ca * sb, sa, sa * cb]
    return np.stack(rows).astype(np.float32)


def cos_sin(index):
    m = jnp.bitwise_and(index, 63) + 8
    quarter = jnp.bitwise_and(jnp.right_shift(m, 4), 3)
    x = (jnp.bitwise_and(m, 15) - 8).astype(F32) * F32(THETA)
    x2 = x * x
    c = 1.0 + x2 * (-0.5 + x2 * (1 / 24 + x2 * (-1 / 720 + x2 * (1 / 40320))))
    s = x * (1.0 + x2 * (-1 / 6 + x2 * (1 / 120 + x2 * (-1 / 5040 + x2 * (1 / 362880)))))
    odd = jnp.bitwise_and(quarter, 1) == 1
    cc = jnp.where(odd, s, c)
    ss = jnp.where(odd, c, s)
    cos = jnp.where((quarter == 1) | (quarter == 2), -cc, cc)
    sin = jnp.where(quarter >= 2, -ss, ss)
    return cos, sin


def split3(value):
    high = value.astype(BF16)
    rest = value - high.astype(F32)
    middle = rest.astype(BF16)
    low = (rest - middle.astype(F32)).astype(BF16)
    return high, middle, low


def dot(a, b, dims):
    return lax.dot_general(a, b, (dims, ((), ())), preferred_element_type=F32)


def ring(i):
    return lax.rem(i + 8, 4)


def kernel(
    images_ref, refs_ref, ctf_ref, noise_ref, ints_ref, views_ref, table_ref,
    sums_ref, weights_ref, norm_ref, peak_ref,
    img, ctf, g_a, g_b, al_a, al_b, wsel, spin, s_a, s_b, mag, gain, en, onehot_t,
    sc, massn, l_a, l_b, rp_a, rp_b,
    st, sb_a, sb_b, rb_a, rb_b, sb2_a, sb2_b, rb2_a, rb2_b, sb3_a, sb3_b, rb3_a, rb3_b,
    load_sem, ag_send, ag_recv, dir_send, dir_recv, rs_send, rs_recv,
):
    g = (g_a, g_b)
    al = (al_a, al_b)
    s_buf = (s_a, s_b)
    l_buf = (l_a, l_b)
    rp = (rp_a, rp_b)
    sb, rb = (sb_a, sb_b), (rb_a, rb_b)
    sb2, rb2 = (sb2_a, sb2_b), (rb2_a, rb2_b)
    sb3, rb3 = (sb3_a, sb3_b), (rb3_a, rb3_b)

    me_dir = lax.axis_index("dir")
    me_dom = lax.axis_index("dom")
    y = me_dom // 8
    z = lax.rem(me_dom // 4, 2)
    x = lax.rem(me_dom, 4)

    def device(yy, zz, xx):
        return (me_dir, (yy * 2 + zz) * 4 + xx)

    x_up, x_down = device(y, z, ring(x + 1)), device(y, z, ring(x - 1))
    y_up, y_down = device(ring(y + 1), z, x), device(ring(y - 1), z, x)
    z_other = device(y, 1 - z, x)
    dir_peers = [(lax.rem(me_dir + o, 8), me_dom) for o in range(1, 8)]

    c2, c1 = (y, x), (x, y)
    up2, down2 = (y_up, x_up), (y_down, x_down)
    up1, down1 = (x_up, y_up), (x_down, y_down)

    def rel(r):
        return lax.rem(z + r, 2)

    load_images = pltpu.make_async_copy(images_ref, img, load_sem.at[0])
    load_images.start()
    load_ctf = pltpu.make_async_copy(ctf_ref, ctf, load_sem.at[1])
    load_ctf.start()

    barrier = pltpu.get_barrier_semaphore()
    partners = [z_other, x_up, x_down, y_up, y_down] + dir_peers
    for p in partners:
        pl.semaphore_signal(barrier, inc=1, device_id=p, device_id_type=MESH)

    for h in range(2):
        real = refs_ref[:, h * HP:(h + 1) * HP].astype(F32)
        imag = refs_ref[:, PIX + h * HP:PIX + (h + 1) * HP].astype(F32)
        g[h][c2[h], z, c1[h]] = jnp.concatenate([real, imag], axis=0).astype(BF16)

    pl.semaphore_wait(barrier, len(partners))

    def ag_copy(h, k, ref, target):
        return pltpu.make_async_remote_copy(
            src_ref=ref, dst_ref=ref, send_sem=ag_send.at[h, k], recv_sem=ag_recv.at[h, k],
            device_id=target, device_id_type=MESH,
        )

    def block(h, r, d):
        return g[h].at[c2[h], rel(r), ring(c1[h] + d)]

    def slab(h, r, d):
        return g[h].at[ring(c2[h] + d), rel(r)]

    def ag(h, k):
        if k == 0:
            return ag_copy(h, k, block(h, 0, 0), z_other)
        if k == 1:
            return ag_copy(h, k, block(h, 0, 0), up1[h])
        if k == 2:
            return ag_copy(h, k, block(h, 1, 0), up1[h])
        if k == 3:
            return ag_copy(h, k, block(h, 0, -1), up1[h])
        if k == 4:
            return ag_copy(h, k, block(h, 0, 0), down1[h])
        if k == 5:
            return ag_copy(h, k, block(h, 1, 0), down1[h])
        if k == 6:
            return ag_copy(h, k, block(h, 1, 1), down1[h])
        if k == 7:
            return ag_copy(h, k, slab(h, 0, 0), up2[h])
        if k == 8:
            return ag_copy(h, k, slab(h, 1, 0), up2[h])
        if k == 9:
            return ag_copy(h, k, slab(h, 0, -1), up2[h])
        if k == 10:
            return ag_copy(h, k, slab(h, 1, 0), down2[h])
        if k == 11:
            return ag_copy(h, k, slab(h, 0, 0), down2[h])
        return ag_copy(h, k, slab(h, 1, 1), down2[h])

    def ag_start(*ks):
        for k in ks:
            for h in range(2):
                ag(h, k).start()

    def ag_wait(*ks):
        for k in ks:
            for h in range(2):
                ag(h, k).wait_recv()

    ag_start(0, 1, 4)

    classes = ints_ref[0:1, :]
    psi_prev = ints_ref[1:2, :]
    ranges = ints_ref[2:3, :]

    def column(row):
        wide = jnp.broadcast_to(row.astype(F32), (128, N))
        return jnp.transpose(wide).astype(jnp.int32)

    shift_y = column(ints_ref[3:4, :])
    shift_x = column(ints_ref[4:5, :])
    lane = lax.broadcasted_iota(jnp.int32, (N, 128), 1)
    fc, fs = cos_sin(
        jnp.bitwise_and(lane, 31) * shift_x + jnp.right_shift(lane, 5) * shift_y
    )
    spin[0], spin[1] = fc, fs
    rc, rs = cos_sin(4 * shift_y)
    spin[2], spin[3] = rc, rs
    qc, qs = cos_sin(16 * shift_y)
    spin[4], spin[5] = qc, qs

    class_rows = lax.broadcasted_iota(jnp.int32, (128, N), 0)
    mask_t = (class_rows == classes).astype(F32)
    onehot_t[...] = mask_t.astype(BF16)
    onehot = jnp.transpose(mask_t).astype(BF16)

    load_ctf.wait()
    noise = noise_ref[...]
    for j in range(8):
        lanes = slice(j * 256, (j + 1) * 256)
        ctf_now = ctf[:, lanes]
        noise_now = noise[:, lanes]
        gain_now = ctf_now * ctf_now / noise_now
        gain[0:GROUPS, lanes] = gain_now
        gain[GROUPS:128, lanes] = jnp.zeros_like(gain_now)
        high, middle, low = split3(ctf_now / noise_now)
        pick = onehot[:, 0:GROUPS]
        wsel[:, lanes] = (
            dot(pick, high, ((1,), (0,))) + dot(pick, middle, ((1,), (0,)))
        ) + dot(pick, low, ((1,), (0,)))

    ag_wait(0)
    ag_start(5, 2)

    load_images.wait()

    def align(part, carry):
        rows = pl.ds(pl.multiple_of(part * 32, 32), 32)
        base_c, base_s = [spin[0, rows]], [spin[1, rows]]
        step_c, step_s = spin[2, rows], spin[3, rows]
        turn_c, turn_s = spin[4, rows], spin[5, rows]
        for j in range(16):
            if j == 0:
                c, s = base_c[0], base_s[0]
            elif j < 4:
                pc, ps = base_c[j - 1], base_s[j - 1]
                c, s = pc * step_c - ps * step_s, ps * step_c + pc * step_s
                base_c.append(c)
                base_s.append(s)
            else:
                pc, ps = base_c[j % 4], base_s[j % 4]
                c, s = pc * turn_c - ps * turn_s, ps * turn_c + pc * turn_s
                base_c[j % 4], base_s[j % 4] = c, s
            lanes = slice(j * 128, (j + 1) * 128)
            real = img[rows, lanes].astype(F32)
            imag = img[rows, PIX + j * 128:PIX + (j + 1) * 128].astype(F32)
            weight = wsel[rows, lanes]
            h, jj = j // 8, j % 8
            al[h][rows, jj * 128:(jj + 1) * 128] = ((real * c + imag * s) * weight).astype(BF16)
            al[h][rows, HP + jj * 128:HP + (jj + 1) * 128] = (
                (imag * c - real * s) * weight
            ).astype(BF16)
        return carry

    lax.fori_loop(0, 3, align, 0)
    ag_wait(1)
    ag_start(3)
    ag_wait(5)
    ag_start(6)
    lax.fori_loop(3, 6, align, 0)
    ag_wait(4, 3)
    ag_start(7, 11)
    ag_wait(2, 6)
    ag_start(10, 8)
    lax.fori_loop(6, 8, align, 0)

    def cross_chunk(h, now):
        for j in range(8):
            lanes = slice(j * 128, (j + 1) * 128)
            wide = slice(h * HP + j * 128, h * HP + (j + 1) * 128)
            value = g[h][now, :, :, :, lanes].astype(F32).reshape(8, 16, 128)
            real, imag = value[:, 0:8], value[:, 8:16]
            mag[:, lanes] = (real * real + imag * imag).reshape(64, 128)

            def put(t, shifted_real, shifted_imag):
                rows = slice(t * 64, (t + 1) * 64)
                s_buf[h][rows, lanes] = shifted_real.reshape(64, 128).astype(BF16)
                s_buf[h][rows, HP + j * 128:HP + (j + 1) * 128] = (
                    shifted_imag.reshape(64, 128).astype(BF16)
                )

            put(4, real, imag)
            for q, (ty, tx) in enumerate(PAIRS):
                c = table_ref[2 * q:2 * q + 1, wide][None]
                s = table_ref[2 * q + 1:2 * q + 2, wide][None]
                rc_, is_, rs_, ic_ = real * c, imag * s, real * s, imag * c
                put(offset_index(ty, tx), rc_ - is_, rs_ + ic_)
                put(offset_index(-ty, -tx), rc_ + is_, ic_ - rs_)
        en[h, now] = lax.dot_general(
            mag[...], gain[:, h * HP:(h + 1) * HP], (((1,), (1,)), ((), ())),
            precision=lax.Precision.HIGHEST, preferred_element_type=F32,
        ).reshape(8, 8, 128)
        sc[h, now] = dot(s_buf[h][...], al[h][...], ((1,), (1,))).reshape(OFFSETS, 8, 8, N)

    def cross_step(i, carry):
        @pl.when(i == 1)
        def _():
            ag_wait(7)
            ag_start(9)
            ag_wait(10)
            ag_start(12)
            ag_wait(8, 11)

        @pl.when(i == 3)
        def _():
            ag_wait(9, 12)

        ahead = lax.rem((i * (i + 1)) // 2, 4)
        for h in range(2):
            cross_chunk(h, ring(c2[h] + ahead))
        return carry

    lax.fori_loop(0, 4, cross_step, 0)

    psi_rows = lax.broadcasted_iota(jnp.int32, (16, N), 0)
    apart = jnp.abs(psi_rows - psi_prev)
    apart = jnp.minimum(apart, 16 - apart).astype(F32)
    psi_term = -(apart * apart * F32(0.5 / 9.0))

    def score_pass(yy, top):
        for zz in range(2):
            for xp in range(2):
                rows = [
                    en[0, yy, zz * 4 + 2 * xp + xx] + en[1, 2 * xp + xx, zz * 4 + yy]
                    for xx in range(2)
                ]
                high, middle, low = split3(jnp.concatenate(rows, axis=0))
                picked = (
                    dot(high, onehot_t[...], ((1,), (0,)))
                    + dot(middle, onehot_t[...], ((1,), (0,)))
                ) + dot(low, onehot_t[...], ((1,), (0,)))
                view = views_ref[yy * 4 + zz * 2 + xp]
                reward = jnp.where(ranges == view, F32(1.5), F32(0.0))
                prior = psi_term + reward
                penalty = 0.5 * picked
                for xx in range(2):
                    part = slice(xx * 8, (xx + 1) * 8)
                    for t in range(OFFSETS):
                        value = (
                            sc[0, yy, t, zz * 4 + 2 * xp + xx]
                            + sc[1, 2 * xp + xx, t, zz * 4 + yy]
                        )
                        value = (value - penalty[part]) + prior[part]
                        sc[0, yy, t, zz * 4 + 2 * xp + xx] = value
                        top = jnp.maximum(top, value)
        return top

    top = lax.fori_loop(0, 4, score_pass, jnp.full((8, N), -jnp.inf, F32))
    top = jnp.max(top, axis=0, keepdims=True)

    def exp_pass(yy, total):
        for t in range(OFFSETS):
            for b in range(8):
                value = jnp.exp(sc[0, yy, t, b] - top)
                sc[0, yy, t, b] = value
                total = total + value
        return total

    total = lax.fori_loop(0, 4, exp_pass, jnp.zeros((8, N), F32))
    total = jnp.sum(total, axis=0, keepdims=True)

    st[me_dir] = jnp.concatenate(
        [jnp.broadcast_to(top, (8, N)), jnp.broadcast_to(total, (8, N))], axis=0
    )

    def dir_copy(o):
        return pltpu.make_async_remote_copy(
            src_ref=st.at[me_dir], dst_ref=st.at[me_dir], send_sem=dir_send.at[o - 1],
            recv_sem=dir_recv.at[o - 1], device_id=dir_peers[o - 1], device_id_type=MESH,
        )

    def dir_arrival(o):
        source = lax.rem(me_dir + 8 - o, 8)
        return pltpu.make_async_remote_copy(
            src_ref=st.at[source], dst_ref=st.at[source], send_sem=dir_send.at[o - 1],
            recv_sem=dir_recv.at[o - 1], device_id=dir_peers[o - 1], device_id_type=MESH,
        )

    for o in range(1, 8):
        dir_copy(o).start()
    for o in range(1, 8):
        dir_arrival(o).wait_recv()

    best = st[0, 0:1]
    for d in range(1, 8):
        best = jnp.maximum(best, st[d, 0:1])
    mass_all = st[0, 8:9] * jnp.exp(st[0, 0:1] - best)
    for d in range(1, 8):
        mass_all = mass_all + st[d, 8:9] * jnp.exp(st[d, 0:1] - best)
    log_norm = best + jnp.log(mass_all)
    norm_ref[...] = log_norm
    peak_ref[...] = jnp.exp(best - log_norm)
    factor = jnp.exp(top - log_norm)

    def posterior_pass(yy, carry):
        for b in range(8):
            p = [
                (sc[0, yy, t, b] * factor).astype(BF16).astype(F32) for t in range(OFFSETS)
            ]
            by_row = []
            for ty in range(3):
                minus, zero, plus = p[3 * ty], p[3 * ty + 1], p[3 * ty + 2]
                by_row.append((zero, plus + minus, plus - minus))
            out = []
            for k in range(3):
                minus, zero, plus = by_row[0][k], by_row[1][k], by_row[2][k]
                out.append((zero, plus + minus, plus - minus))
            order = (
                out[0][0], out[1][0], out[0][1], out[1][1], out[2][2],
                out[2][0], out[2][1], out[0][2], out[1][2],
            )
            for k in range(OFFSETS):
                sc[1, yy, k, b] = order[k]
            massn[yy, b] = (out[0][0] + out[1][0]) + (out[0][1] + out[1][1])
        return carry

    lax.fori_loop(0, 4, posterior_pass, 0)

    def insert_chunk(h, i, now):
        for zz in range(2):
            for cp in range(2):
                pair = []
                for c in range(2):
                    cc = 2 * cp + c
                    if h == 0:
                        pair.append(sc[1, now, :, zz * 4 + cc])
                    else:
                        pair.append(sc[1, cc, :, zz * 4 + now])
                l_buf[h][:, zz * 2 + cp] = jnp.concatenate(pair, axis=1).astype(BF16)
        left = l_buf[h][...].reshape(OFFSETS * 64, N)
        for q in range(4):
            lanes = slice(q * 256, (q + 1) * 256)
            wide = slice(h * HP + q * 256, h * HP + (q + 1) * 256)
            real = dot(left, al[h][:, lanes], ((1,), (0,))).reshape(OFFSETS, 64, 256)
            imag = dot(
                left, al[h][:, HP + q * 256:HP + (q + 1) * 256], ((1,), (0,))
            ).reshape(OFFSETS, 64, 256)
            total_real, total_imag = real[0], imag[0]
            for k in range(4):
                w = table_ref[8 + k:9 + k, wide]
                total_real = total_real + w * real[1 + k]
                total_imag = total_imag + w * imag[1 + k]
            for k in range(4):
                w = table_ref[12 + k:13 + k, wide]
                total_real = total_real + w * imag[5 + k]
                total_imag = total_imag - w * real[5 + k]
            rp[h][i, :, 0:8, lanes] = total_real.reshape(8, 8, 256)
            rp[h][i, :, 8:16, lanes] = total_imag.reshape(8, 8, 256)
        if h == 0:
            high, middle, _ = split3(massn[now].reshape(64, N))
            masses = dot(high, onehot_t[...], ((1,), (1,))) + dot(
                middle, onehot_t[...], ((1,), (1,))
            )
            rp[h][i, :, 0:8, HP:HP + 128] = masses.reshape(8, 8, 128)
            rp[h][i, :, 8:16, HP:HP + 128] = jnp.zeros((8, 8, 128), F32)

    def rs_copy(h, k, src, dst, target):
        return pltpu.make_async_remote_copy(
            src_ref=src, dst_ref=dst, send_sem=rs_send.at[h, k], recv_sem=rs_recv.at[h, k],
            device_id=target, device_id_type=MESH,
        )

    def rs(h, k):
        if k < 6:
            target = up2[h] if k < 3 else down2[h]
            return rs_copy(h, k, sb[h].at[k], rb[h].at[k], target)
        if k < 12:
            target = up1[h] if k < 9 else down1[h]
            return rs_copy(h, k, sb2[h].at[k - 6], rb2[h].at[k - 6], target)
        return rs_copy(h, k, sb3[h], rb3[h], z_other)

    def send_half(h, k, i, zz, add=None):
        part = rp[h][i, zz * 4:(zz + 1) * 4]
        if add is not None:
            part = part + rb[h][add].astype(F32)
        sb[h][k] = part.astype(BF16)
        rs(h, k).start()

    def insert_step(i, carry):
        back = 3 - i
        ahead = lax.rem((back * (back + 1)) // 2, 4)
        for h in range(2):
            insert_chunk(h, i, ring(c2[h] + ahead))

            @pl.when(i == 0)
            def _():
                send_half(h, 0, 0, 0)
                send_half(h, 3, 0, 1)

            @pl.when(i == 1)
            def _():
                send_half(h, 4, 1, 0)

            @pl.when(i == 2)
            def _():
                send_half(h, 1, 2, 1)
                rs(h, 0).wait_recv()
                send_half(h, 2, 2, 0, add=0)
                rs(h, 3).wait_recv()
                send_half(h, 5, 1, 1, add=3)

        return carry

    lax.fori_loop(0, 4, insert_step, 0)

    for h in range(2):
        for k in (1, 2, 4, 5):
            rs(h, k).wait_recv()
        for zz, (from_below, from_above) in enumerate(((2, 4), (1, 5))):
            part = slice(zz * 4, (zz + 1) * 4)
            rp[h][3, part] = (
                rp[h][3, part] + rb[h][from_below].astype(F32)
            ) + rb[h][from_above].astype(F32)

        far, above, below = ring(c1[h] + 2), ring(c1[h] + 1), ring(c1[h] - 1)
        for k, zz, cc in ((6, 0, far), (9, 1, far), (7, 1, above), (10, 0, below)):
            sb2[h][k - 6] = rp[h][3, zz * 4 + cc].astype(BF16)
            rs(h, k).start()

    for h in range(2):
        far, above, below = ring(c1[h] + 2), ring(c1[h] + 1), ring(c1[h] - 1)
        for k, zz, cc, add in ((8, 0, above, 6), (11, 1, below, 9)):
            rs(h, add).wait_recv()
            sb2[h][k - 6] = (
                rp[h][3, zz * 4 + cc] + rb2[h][add - 6].astype(F32)
            ).astype(BF16)
            rs(h, k).start()

    own = []
    for h in range(2):
        for k in (7, 8, 10, 11):
            rs(h, k).wait_recv()
        sums = []
        for zz, (from_below, from_above) in enumerate(((8, 10), (7, 11))):
            sums.append(
                (rp[h][3, zz * 4 + c1[h]] + rb2[h][from_below - 6].astype(F32))
                + rb2[h][from_above - 6].astype(F32)
            )
        is_low = z == 0
        mine = jnp.where(is_low, sums[0], sums[1])
        sb3[h][...] = jnp.where(is_low, sums[1], sums[0]).astype(BF16)
        rs(h, 12).start()
        own.append(mine)

    for h in range(2):
        rs(h, 12).wait_recv()
        result = own[h] + rb3[h][...].astype(F32)
        sums_ref[:, h * HP:(h + 1) * HP] = result[0:8, 0:HP]
        sums_ref[:, PIX + h * HP:PIX + (h + 1) * HP] = result[8:16, 0:HP]
        if h == 0:
            weights_ref[...] = lax.dot_general(
                result[0:8, HP:HP + 128], gain[...], (((1,), (0,)), ((), ())),
                precision=lax.Precision.HIGHEST, preferred_element_type=F32,
            )

    for h in range(2):
        for k in range(13):
            ag(h, k).wait_send()
            rs(h, k).wait_send()
    for o in range(1, 8):
        dir_copy(o).wait_send()


def per_device(
    images, refs, ctf, noise_var, shifts, ctf_class, psi_prev, earlier_direction_range, view_range
):
    ints = jnp.stack(
        [ctf_class, psi_prev, earlier_direction_range, shifts[:, 0], shifts[:, 1]]
    )
    vmem = pl.BlockSpec(memory_space=pltpu.VMEM)
    hbm = pl.BlockSpec(memory_space=pl.ANY)
    smem = pl.BlockSpec(memory_space=pltpu.SMEM)
    wa, wb = WIDTHS
    dma = pltpu.SemaphoreType.DMA
    out = pl.pallas_call(
        kernel,
        out_shape=(
            jax.ShapeDtypeStruct((8, 2 * PIX), F32),
            jax.ShapeDtypeStruct((8, PIX), F32),
            jax.ShapeDtypeStruct((1, N), F32),
            jax.ShapeDtypeStruct((1, N), F32),
        ),
        in_specs=[hbm, vmem, hbm, vmem, vmem, smem, vmem],
        out_specs=(vmem, vmem, vmem, vmem),
        scratch_shapes=[
            pltpu.VMEM((N, 2 * PIX), BF16),
            pltpu.VMEM((GROUPS, PIX), F32),
            pltpu.VMEM((4, 2, 4, 16, HP), BF16),
            pltpu.VMEM((4, 2, 4, 16, HP), BF16),
            pltpu.VMEM((N, 2 * HP), BF16),
            pltpu.VMEM((N, 2 * HP), BF16),
            pltpu.VMEM((N, PIX), F32),
            pltpu.VMEM((6, N, 128), F32),
            pltpu.VMEM((OFFSETS * 64, 2 * HP), BF16),
            pltpu.VMEM((OFFSETS * 64, 2 * HP), BF16),
            pltpu.VMEM((64, HP), F32),
            pltpu.VMEM((128, PIX), F32),
            pltpu.VMEM((2, 4, 8, 8, 128), F32),
            pltpu.VMEM((128, N), BF16),
            pltpu.VMEM((2, 4, OFFSETS, 8, 8, N), F32),
            pltpu.VMEM((4, 8, 8, N), F32),
            pltpu.VMEM((OFFSETS, 4, 16, N), BF16),
            pltpu.VMEM((OFFSETS, 4, 16, N), BF16),
            pltpu.VMEM((4, 8, 16, wa), F32),
            pltpu.VMEM((4, 8, 16, wb), F32),
            pltpu.VMEM((8, 16, N), F32),
            pltpu.VMEM((6, 4, 16, wa), BF16),
            pltpu.VMEM((6, 4, 16, wb), BF16),
            pltpu.VMEM((6, 4, 16, wa), BF16),
            pltpu.VMEM((6, 4, 16, wb), BF16),
            pltpu.VMEM((6, 16, wa), BF16),
            pltpu.VMEM((6, 16, wb), BF16),
            pltpu.VMEM((6, 16, wa), BF16),
            pltpu.VMEM((6, 16, wb), BF16),
            pltpu.VMEM((16, wa), BF16),
            pltpu.VMEM((16, wb), BF16),
            pltpu.VMEM((16, wa), BF16),
            pltpu.VMEM((16, wb), BF16),
            dma((2,)),
            dma((2, 13)),
            dma((2, 13)),
            dma((7,)),
            dma((7,)),
            dma((2, 13)),
            dma((2, 13)),
        ],
        compiler_params=pltpu.CompilerParams(
            collective_id=0, has_side_effects=True, vmem_limit_bytes=60 * 2**20
        ),
        cost_estimate=pl.CostEstimate(
            flops=10_000_000_000, bytes_accessed=4_000_000, transcendentals=600_000
        ),
        name="expectation_step",
    )(
        images, refs, ctf, noise_var.reshape(1, PIX), ints, view_range,
        jnp.asarray(phase_constants()),
    )
    class_sums, weight_sums, log_norm, peak_prob = out
    return class_sums, weight_sums, log_norm.reshape(N), peak_prob.reshape(N)


def solution(mesh):
    placed = (
        P("dom", None),
        P(("dir", "dom"), None),
        P(),
        P(),
        P("dom", None),
        P("dom"),
        P("dom"),
        P("dom"),
        P("dir"),
    )
    return jax.shard_map(
        per_device,
        mesh=mesh,
        in_specs=placed,
        out_specs=(P(("dir", "dom"), None), P(("dir", "dom"), None), P("dom"), P("dom")),
        check_vma=False,
    )
```

time: 717 us -> 76 us (0.11)
  waiting for transfers between devices: 517 us -> 0 us
  Pallas kernels: 0 us -> 66.9 us
  other arithmetic: 60.8 us -> 0 us
  local copies, waits for them, and re-layouts: 60.6 us -> 7.51 us
  blocking collectives: 29.2 us -> 0 us
  matrix products: 27.8 us -> 0 us
  between operations: 14.5 us -> 0.64 us
    unnamed x4 -> x0, waiting for transfers between devices: 208 us -> none
    reduce_scatter x1 -> x0, waiting for transfers between devices: 166 us -> none  [per_device(): lax.psum_scatter(insert_images(posterior, aligned, offset_cos, offset_sin...]
    all_gather x1 -> x0, waiting for transfers between devices: 143 us -> none  [per_device(): piece = lax.all_gather(refs, 'dom', axis=0, tiled=True)]
    pallas_call x0 -> x1, Pallas kernels: none -> 66.9 us  [per_device(): pl.pallas_call(kernel, out_shape=(jax.ShapeDtypeStruct((8, 2 * PIX), F32)...]
    while x36 -> x0, local copies, waits for them, and re-layouts: 31.9 us -> none
    another operation x10 -> x0, other arithmetic: 31.1 us -> none
    dot_general x21 -> x0, matrix products: 27.8 us -> none  [the longest x9 14.8 us: add_offset(): lax.dot_general(weights_now, aligned, (((0,), (0,)), ((), ())), preferred...]
    add x18 -> x0, other arithmetic: 17.9 us -> none  [the longest x9 12.7 us: add_offset(): return total + turned]
  transfers between devices with their start and end apart: 3 -> 0, of which waited for: 3 -> 0; matrix products, arithmetic and copies ran while one was open for 8% -> 0% of each run, Pallas kernels for 0% -> 0%
where the time goes in v1:
time: 76 us; the launch traced here: 75.1 us
  Pallas kernels  66.9 us (88%)
  local copies, waits for them, and re-layouts  7.51 us (10%)
    pallas_call x1, Pallas kernels, per_device(): pl.pallas_call(kernel, out_shape=(jax.ShapeDtypeStruct((8, 2 * PIX), F32)...  66.9 us
    unnamed x4, local copies, waits for them, and re-layouts  5.43 us
    another operation x2, local copies, waits for them, and re-layouts, per_device(): jnp.stack([ctf_class, psi_prev, earlier_direction_range, shifts[:, 0], sh...  2.08 us

profile of v1, /device:TPU:2, one launch (start us, length us, event | category | flops | bytes accessed | tf_op | source)
XLA Modules:
  0.0 75.1 jit_solution(15238075954304442983)
XLA Ops:
  0.6 0.8 %slice_bitcast_fusion = (s32[1,256]{1,0:T(1,128)S(1)}, s32[1,256]{1,0:T(1,128)S(1)}) fusion(s32[256,2]{0,1:T(2,128)} %param.14), kind=kLoop, calls=%fused_computation | loop fusion | bytes 4096 | tf_op jit(solution)/shard_map/stack;squeeze | solution.py:568
  1.4 1.3 %stack.15.ints_ref = s32[5,256]{1,0:T(8,128)} concatenate(s32[1,256]{1,0:T(1,128)} %bitcast.12, s32[1,256]{1,0:T(1,128)} %bitcast.13, s32[1,256]{1,0:T(1,128)} %bitcast.14, s32[1,256]{1,0:T(1,128)S(1)} %get-tuple-element.13, s32[1,256]{1,0:T(1,128)S(1)} %get-tuple-element.12), dimensions={0} | concatenate | bytes 10240 | tf_op jit(solution)/shard_map/stack | solution.py:568
  2.7 66.9 %expectation_step.1 = (f32[8,4096]{1,0:T(8,128)}, f32[8,2048]{1,0:T(8,128)}, f32[1,256]{1,0:T(1,128)}, f32[1,256]{1,0:T(1,128)}) custom-call(bf16[256,4096]{1,0:T(8,128)(2,1)} %images_ref.1, bf16[8,4096]{1,0:T(8,128)(2,1)} %refs_ref.1, f32[64,2048]{1,0:T(8,128)} %ctf_ref.1, f32[1,2048]{1,0:T(1,128)} %bitcast.15, s32[5,256]{1,0:T(8,128)} %stack.15.ints_ref, ...), custom_call_target="tpu_custom_call" | custom-call | flops 10000000000 | bytes 4000000 | tf_op jit(solution)/shard_map/expectation_step/pallas_call | solution.py:576
  69.7 1.6 %copy.18 = f32[8,4096]{1,0:T(8,128)} copy(f32[8,4096]{1,0:T(8,128)} %get-tuple-element.18) | data formatting | bytes 262144
  71.2 1.5 %copy.19 = f32[8,2048]{1,0:T(8,128)} copy(f32[8,2048]{1,0:T(8,128)} %get-tuple-element.19) | data formatting | bytes 131072
  72.7 1.2 %copy.20 = f32[256]{0:T(256)} copy(f32[256]{0:T(256)} %bitcast.11) | data formatting | bytes 2048
  73.9 1.2 %copy.21 = f32[256]{0:T(256)} copy(f32[256]{0:T(256)} %bitcast.10) | data formatting | bytes 2048

commit v2 on v1

v2 whole, which is shorter than its diff:
```python
import math

import jax
import jax.numpy as jnp
import numpy as np
from jax import lax
from jax.experimental import pallas as pl
from jax.experimental.pallas import tpu as pltpu
from jax.sharding import PartitionSpec as P

CROP = 64
HALF = 32
PIX = 2048
OFFSETS = 9
GROUPS = 64
N = 256
BLOCKS = 32
HP = 1024
WIDTHS = (HP + 128, HP)
THETA = 2.0 * math.pi / CROP

F32 = jnp.float32
BF16 = jnp.bfloat16
MESH = pl.DeviceIdType.MESH

PAIRS = ((0, 1), (1, 0), (1, 1), (1, -1))


def offset_index(ty, tx):
    return (ty + 1) * 3 + (tx + 1)


def phase_constants():
    pixels = np.arange(PIX)
    alpha = THETA * (pixels // HALF)
    beta = THETA * (pixels % HALF)
    rows = []
    for ty, tx in PAIRS:
        angle = ty * alpha + tx * beta
        rows += [np.cos(angle), np.sin(angle)]
    ca, sa, cb, sb = np.cos(alpha), np.sin(alpha), np.cos(beta), np.sin(beta)
    rows += [cb, ca, ca * cb, -sa * sb, sb, ca * sb, sa, sa * cb]
    return np.stack(rows).astype(np.float32)


def cos_sin(index):
    m = jnp.bitwise_and(index, 63) + 8
    quarter = jnp.bitwise_and(jnp.right_shift(m, 4), 3)
    x = (jnp.bitwise_and(m, 15) - 8).astype(F32) * F32(THETA)
    x2 = x * x
    c = 1.0 + x2 * (-0.5 + x2 * (1 / 24 + x2 * (-1 / 720 + x2 * (1 / 40320))))
    s = x * (1.0 + x2 * (-1 / 6 + x2 * (1 / 120 + x2 * (-1 / 5040 + x2 * (1 / 362880)))))
    odd = jnp.bitwise_and(quarter, 1) == 1
    cc = jnp.where(odd, s, c)
    ss = jnp.where(odd, c, s)
    cos = jnp.where((quarter == 1) | (quarter == 2), -cc, cc)
    sin = jnp.where(quarter >= 2, -ss, ss)
    return cos, sin


def split3(value):
    high = value.astype(BF16)
    rest = value - high.astype(F32)
    middle = rest.astype(BF16)
    low = (rest - middle.astype(F32)).astype(BF16)
    return high, middle, low


def dot(a, b, dims):
    return lax.dot_general(a, b, (dims, ((), ())), preferred_element_type=F32)


def ring(i):
    return lax.rem(i + 8, 4)


def ahead_of(place):
    return lax.rem((place * (place + 1)) // 2, 4)


PIECES = (slice(0, 1), slice(1, 3), slice(3, 4))
PARTS = (slice(1, 4), slice(0, 1))


def kernel(
    images_ref, refs_ref, ctf_ref, noise_ref, class_ref, psi_ref, range_ref, shift_ref,
    views_ref, table_in,
    sums_ref, weights_ref, stats_ref,
    img, refs_in, ctf, noise_in, ints, shift_in, table_ref,
    g_a, g_b, al_a, al_b, wsel, spin, s_a, s_b, mag, gain, gain3, en, onehot_t, psi_rows_sc,
    sc, massn, l_a, l_b, rp_a, rp_b,
    st, sb_a, sb_b, rb_a, rb_b, sb2_a, sb2_b, rb2_a, rb2_b, sb3_a, sb3_b, rb3_a, rb3_b,
    load_sem, ag_send, ag_recv, dir_send, dir_recv, rs_send, rs_recv,
):
    g = (g_a, g_b)
    al = (al_a, al_b)
    s_buf = (s_a, s_b)
    l_buf = (l_a, l_b)
    rp = (rp_a, rp_b)
    sb, rb = (sb_a, sb_b), (rb_a, rb_b)
    sb2, rb2 = (sb2_a, sb2_b), (rb2_a, rb2_b)
    sb3, rb3 = (sb3_a, sb3_b), (rb3_a, rb3_b)

    me_dir = lax.axis_index("dir")
    me_dom = lax.axis_index("dom")
    y = me_dom // 8
    z = lax.rem(me_dom // 4, 2)
    x = lax.rem(me_dom, 4)

    def device(yy, zz, xx):
        return (me_dir, (yy * 2 + zz) * 4 + xx)

    x_up, x_down = device(y, z, ring(x + 1)), device(y, z, ring(x - 1))
    y_up, y_down = device(ring(y + 1), z, x), device(ring(y - 1), z, x)
    z_other = device(y, 1 - z, x)
    dir_peers = [(lax.rem(me_dir + o, 8), me_dom) for o in range(1, 8)]

    up2, down2 = (y_up, x_up), (y_down, x_down)
    up1, down1 = (x_up, y_up), (x_down, y_down)

    barrier = pltpu.get_barrier_semaphore()
    partners = [z_other, x_up, x_down, y_up, y_down] + dir_peers
    for p in partners:
        pl.semaphore_signal(barrier, inc=1, device_id=p, device_id_type=MESH)

    loads = [
        pltpu.make_async_copy(src, dst, load_sem.at[k])
        for k, (src, dst) in enumerate((
            (refs_ref, refs_in), (shift_ref, shift_in), (class_ref, ints.at[0:1]),
            (psi_ref, ints.at[1:2]), (range_ref, ints.at[2:3]), (noise_ref, noise_in),
            (ctf_ref, ctf), (images_ref, img), (table_in, table_ref),
        ))
    ]
    for load in loads:
        load.start()

    loads[0].wait()
    for h in range(2):
        real = refs_in[:, h * HP:(h + 1) * HP].astype(F32)
        imag = refs_in[:, PIX + h * HP:PIX + (h + 1) * HP].astype(F32)
        g[h][0, 0, 0] = jnp.concatenate([real, imag], axis=0).astype(BF16)

    pl.semaphore_wait(barrier, len(partners))

    def ag(h, k):
        buf = g[h]
        if k == 0:
            src, dst, target = buf.at[0, 0, 0], buf.at[0, 1, 0], z_other
        elif k < 7:
            kind = (k - 1) % 3
            upward = k < 4
            target = up1[h] if upward else down1[h]
            side = 2 if upward else 1
            if kind < 2:
                src, dst = buf.at[0, kind, 0], buf.at[0, kind, side]
            else:
                r = 0 if upward else 1
                src, dst = buf.at[0, r, side], buf.at[0, r, 3]
        else:
            piece = PIECES[(k - 7) % 3]
            kind = (k - 7) // 3
            upward = kind < 3
            target = up2[h] if upward else down2[h]
            side = 2 if upward else 1
            if kind % 3 < 2:
                r = kind % 3
                src, dst = buf.at[0, r, piece], buf.at[side, r, piece]
            else:
                r = 0 if upward else 1
                src, dst = buf.at[side, r, piece], buf.at[3, r, piece]
        return pltpu.make_async_remote_copy(
            src_ref=src, dst_ref=dst, send_sem=ag_send.at[h, k], recv_sem=ag_recv.at[h, k],
            device_id=target, device_id_type=MESH,
        )

    def ag_start(*ks):
        for k in ks:
            for h in range(2):
                ag(h, k).start()

    def ag_wait(*ks):
        for k in ks:
            for h in range(2):
                ag(h, k).wait_recv()

    Z_, UP, DOWN = 0, (1, 2, 3), (4, 5, 6)

    def outer(kind, piece):
        return 7 + 3 * kind + piece

    U0, U1, UR, D0, D1, DR = range(6)

    ag_start(Z_, UP[0], DOWN[0])
    ag_start(outer(U0, 0), outer(D0, 0))

    for k in range(1, 7):
        loads[k].wait()
    classes = ints[0:1, :]
    psi_prev = ints[1:2, :]
    ranges = ints[2:3, :]

    def column(row):
        wide = jnp.broadcast_to(row.astype(F32), (128, N))
        return jnp.transpose(wide).astype(jnp.int32)

    shift_y = column(shift_in[0:1, :])
    shift_x = column(shift_in[1:2, :])
    lane = lax.broadcasted_iota(jnp.int32, (N, 128), 1)
    fc, fs = cos_sin(
        jnp.bitwise_and(lane, 31) * shift_x + jnp.right_shift(lane, 5) * shift_y
    )
    spin[0], spin[1] = fc, fs
    rc, rs_ = cos_sin(4 * shift_y)
    spin[2], spin[3] = rc, rs_
    qc, qs = cos_sin(16 * shift_y)
    spin[4], spin[5] = qc, qs

    class_rows = lax.broadcasted_iota(jnp.int32, (128, N), 0)
    mask_t = (class_rows == classes).astype(F32)
    onehot_t[...] = mask_t.astype(BF16)
    onehot = jnp.transpose(mask_t).astype(BF16)

    psi_rows = lax.broadcasted_iota(jnp.int32, (16, N), 0)
    apart = jnp.abs(psi_rows - psi_prev)
    apart = jnp.minimum(apart, 16 - apart).astype(F32)
    psi_term = -(apart * apart * F32(0.5 / 9.0))
    psi_rows_sc[0] = psi_term[0:8]
    psi_rows_sc[1] = psi_term[8:16]

    ag_wait(Z_)
    ag_start(UP[1], DOWN[1])
    ag_start(outer(U1, 0), outer(D1, 0))

    noise = noise_in[...]
    for j in range(8):
        lanes = slice(j * 256, (j + 1) * 256)
        ctf_now = ctf[:, lanes]
        noise_now = noise[:, lanes]
        gain_now = ctf_now * ctf_now / noise_now
        gain[:, lanes] = gain_now
        for k, piece in enumerate(split3(gain_now)):
            gain3[k, :, lanes] = piece
        high, middle, low = split3(ctf_now / noise_now)
        pick = onehot[:, 0:GROUPS]
        wsel[:, lanes] = (
            dot(pick, high, ((1,), (0,))) + dot(pick, middle, ((1,), (0,)))
        ) + dot(pick, low, ((1,), (0,)))

    loads[7].wait()
    loads[8].wait()

    ag_wait(UP[0])
    ag_start(UP[2])
    ag_wait(DOWN[0])
    ag_start(outer(U0, 1), outer(D0, 1))

    def align(part, carry):
        rows = pl.ds(pl.multiple_of(part * 32, 32), 32)
        base_c, base_s = [spin[0, rows]], [spin[1, rows]]
        step_c, step_s = spin[2, rows], spin[3, rows]
        turn_c, turn_s = spin[4, rows], spin[5, rows]
        for j in range(16):
            if j == 0:
                c, s = base_c[0], base_s[0]
            elif j < 4:
                pc, ps = base_c[j - 1], base_s[j - 1]
                c, s = pc * step_c - ps * step_s, ps * step_c + pc * step_s
                base_c.append(c)
                base_s.append(s)
            else:
                pc, ps = base_c[j % 4], base_s[j % 4]
                c, s = pc * turn_c - ps * turn_s, ps * turn_c + pc * turn_s
                base_c[j % 4], base_s[j % 4] = c, s
            lanes = slice(j * 128, (j + 1) * 128)
            real = img[rows, lanes].astype(F32)
            imag = img[rows, PIX + j * 128:PIX + (j + 1) * 128].astype(F32)
            weight = wsel[rows, lanes]
            h, jj = j // 8, j % 8
            al[h][rows, jj * 128:(jj + 1) * 128] = ((real * c + imag * s) * weight).astype(BF16)
            al[h][rows, HP + jj * 128:HP + (jj + 1) * 128] = (
                (imag * c - real * s) * weight
            ).astype(BF16)
        return carry

    lax.fori_loop(0, 4, align, 0)
    ag_wait(outer(U0, 0))
    ag_start(outer(UR, 0))
    ag_wait(DOWN[1])
    ag_start(DOWN[2])
    ag_wait(UP[1])
    ag_start(outer(D1, 1), outer(U1, 1))
    ag_wait(outer(D1, 0))
    ag_start(outer(DR, 0))
    lax.fori_loop(4, 8, align, 0)
    ag_wait(UP[2])
    ag_start(outer(U0, 2), outer(D0, 2))
    ag_wait(DOWN[2])
    ag_start(outer(D1, 2), outer(U1, 2))

    def cross_chunk(h, now):
        for j in range(8):
            lanes = slice(j * 128, (j + 1) * 128)
            wide = slice(h * HP + j * 128, h * HP + (j + 1) * 128)
            value = g[h][now, :, :, :, lanes].astype(F32).reshape(8, 16, 128)
            real, imag = value[:, 0:8], value[:, 8:16]
            mag[:, lanes] = (real * real + imag * imag).reshape(64, 128)

            def put(t, shifted_real, shifted_imag):
                rows = slice(t * 64, (t + 1) * 64)
                s_buf[h][rows, lanes] = shifted_real.reshape(64, 128).astype(BF16)
                s_buf[h][rows, HP + j * 128:HP + (j + 1) * 128] = (
                    shifted_imag.reshape(64, 128).astype(BF16)
                )

            put(4, real, imag)
            for q, (ty, tx) in enumerate(PAIRS):
                c = table_ref[2 * q:2 * q + 1, wide][None]
                s = table_ref[2 * q + 1:2 * q + 2, wide][None]
                rc_, is_, rs_, ic_ = real * c, imag * s, real * s, imag * c
                put(offset_index(ty, tx), rc_ - is_, rs_ + ic_)
                put(offset_index(-ty, -tx), rc_ + is_, ic_ - rs_)
        high, middle, low = split3(mag[...])
        half = slice(h * HP, (h + 1) * HP)
        by_high = dot(jnp.concatenate([high, middle, low], axis=0), gain3[0, :, half], ((1,), (1,)))
        by_middle = dot(jnp.concatenate([high, middle], axis=0), gain3[1, :, half], ((1,), (1,)))
        by_low = dot(high, gain3[2, :, half], ((1,), (1,)))
        small = (by_low + by_high[128:192]) + by_middle[64:128]
        energy = (small + (by_middle[0:64] + by_high[64:128])) + by_high[0:64]
        en[h, now, :, :, 0:GROUPS] = energy.reshape(8, 8, GROUPS)
        sc[h, now] = dot(s_buf[h][...], al[h][...], ((1,), (1,))).reshape(OFFSETS, 8, 8, N)

    def cross_step(i, carry):
        @pl.when(i == 1)
        def _():
            ag_wait(outer(U0, 1))
            ag_start(outer(UR, 1))
            ag_wait(outer(D1, 1))
            ag_start(outer(DR, 1))
            ag_wait(outer(U0, 2))
            ag_start(outer(UR, 2))
            ag_wait(outer(D1, 2))
            ag_start(outer(DR, 2))
            ag_wait(outer(D0, 0), outer(D0, 1), outer(D0, 2))

        @pl.when(i == 2)
        def _():
            ag_wait(outer(U1, 0), outer(U1, 1), outer(U1, 2))

        @pl.when(i == 3)
        def _():
            for p in range(3):
                ag_wait(outer(UR, p), outer(DR, p))

        for h in range(2):
            cross_chunk(h, i)
        return carry

    lax.fori_loop(0, 4, cross_step, 0)

    def score_pass(py, top):
        energies = [
            en[0, py, r * 4 + px, :, 0:GROUPS] + en[1, px, r * 4 + py, :, 0:GROUPS]
            for r in range(2) for px in range(4)
        ]
        high, middle, low = split3(jnp.concatenate(energies, axis=0))
        picks = onehot_t[0:GROUPS]
        picked = (
            dot(high, picks, ((1,), (0,))) + dot(middle, picks, ((1,), (0,)))
        ) + dot(low, picks, ((1,), (0,)))
        penalty = 0.5 * picked
        owner_y = ring(y + ahead_of(py))
        for r in range(2):
            owner_z = lax.rem(z + r, 2)
            for px in range(4):
                owner_x = ring(x + (0, 1, 3, 2)[px])
                view = views_ref[owner_y * 4 + owner_z * 2 + owner_x // 2]
                prior = psi_rows_sc[lax.rem(owner_x, 2)] + jnp.where(
                    ranges == view, F32(1.5), F32(0.0)
                )
                b = r * 4 + px
                less = penalty[b * 8:(b + 1) * 8]
                for t in range(OFFSETS):
                    value = sc[0, py, t, b] + sc[1, px, t, r * 4 + py]
                    value = (value - less) + prior
                    sc[0, py, t, b] = value
                    top = jnp.maximum(top, value)
        return top

    top = lax.fori_loop(0, 4, score_pass, jnp.full((8, N), -jnp.inf, F32))
    top = jnp.max(top, axis=0, keepdims=True)

    def exp_pass(yy, total):
        for t in range(OFFSETS):
            for b in range(8):
                value = jnp.exp(sc[0, yy, t, b] - top)
                sc[0, yy, t, b] = value
                total = total + value
        return total

    total = lax.fori_loop(0, 4, exp_pass, jnp.zeros((8, N), F32))
    total = jnp.sum(total, axis=0, keepdims=True)

    for half in range(2):
        lanes = slice(half * 128, (half + 1) * 128)
        st[me_dir, half:half + 1] = top[:, lanes]
        st[me_dir, 2 + half:3 + half] = total[:, lanes]

    def dir_copy(o):
        return pltpu.make_async_remote_copy(
            src_ref=st.at[me_dir], dst_ref=st.at[me_dir], send_sem=dir_send.at[o - 1],
            recv_sem=dir_recv.at[o - 1], device_id=dir_peers[o - 1], device_id_type=MESH,
        )

    def dir_arrival(o):
        source = lax.rem(me_dir + 8 - o, 8)
        return pltpu.make_async_remote_copy(
            src_ref=st.at[source], dst_ref=st.at[source], send_sem=dir_send.at[o - 1],
            recv_sem=dir_recv.at[o - 1], device_id=dir_peers[o - 1], device_id_type=MESH,
        )

    for o in range(1, 8):
        dir_copy(o).start()
    for o in range(1, 8):
        dir_arrival(o).wait_recv()

    def joined(d, row):
        return jnp.concatenate([st[d, row:row + 1], st[d, row + 1:row + 2]], axis=1)

    tops = [joined(d, 0) for d in range(8)]
    best = tops[0]
    for d in range(1, 8):
        best = jnp.maximum(best, tops[d])
    mass_all = joined(0, 2) * jnp.exp(tops[0] - best)
    for d in range(1, 8):
        mass_all = mass_all + joined(d, 2) * jnp.exp(tops[d] - best)
    log_norm = best + jnp.log(mass_all)
    stats_ref[0:1] = log_norm
    stats_ref[1:2] = jnp.exp(best - log_norm)
    factor = jnp.exp(top - log_norm)

    def posterior_pass(yy, carry):
        for b in range(8):
            p = [
                (sc[0, yy, t, b] * factor).astype(BF16).astype(F32) for t in range(OFFSETS)
            ]
            by_row = []
            for ty in range(3):
                minus, zero, plus = p[3 * ty], p[3 * ty + 1], p[3 * ty + 2]
                by_row.append((zero, plus + minus, plus - minus))
            out = []
            for k in range(3):
                minus, zero, plus = by_row[0][k], by_row[1][k], by_row[2][k]
                out.append((zero, plus + minus, plus - minus))
            order = (
                out[0][0], out[1][0], out[0][1], out[1][1], out[2][2],
                out[2][0], out[2][1], out[0][2], out[1][2],
            )
            for k in range(OFFSETS):
                sc[1, yy, k, b] = order[k]
            massn[yy, b] = (out[0][0] + out[1][0]) + (out[0][1] + out[1][1])
        return carry

    lax.fori_loop(0, 4, posterior_pass, 0)

    def insert_chunk(h, now):
        for zz in range(2):
            for cp in range(2):
                pair = []
                for c in range(2):
                    cc = 2 * cp + c
                    if h == 0:
                        pair.append(sc[1, now, :, zz * 4 + cc])
                    else:
                        pair.append(sc[1, cc, :, zz * 4 + now])
                l_buf[h][:, zz * 2 + cp] = jnp.concatenate(pair, axis=1).astype(BF16)
        left = l_buf[h][...].reshape(OFFSETS * 64, N)
        for q in range(4):
            lanes = slice(q * 256, (q + 1) * 256)
            wide = slice(h * HP + q * 256, h * HP + (q + 1) * 256)
            real = dot(left, al[h][:, lanes], ((1,), (0,))).reshape(OFFSETS, 64, 256)
            imag = dot(
                left, al[h][:, HP + q * 256:HP + (q + 1) * 256], ((1,), (0,))
            ).reshape(OFFSETS, 64, 256)
            total_real, total_imag = real[0], imag[0]
            for k in range(4):
                w = table_ref[8 + k:9 + k, wide]
                total_real = total_real + w * real[1 + k]
                total_imag = total_imag + w * imag[1 + k]
            for k in range(4):
                w = table_ref[12 + k:13 + k, wide]
                total_real = total_real + w * imag[5 + k]
                total_imag = total_imag - w * real[5 + k]
            rp[h][now, :, 0:8, lanes] = total_real.reshape(8, 8, 256)
            rp[h][now, :, 8:16, lanes] = total_imag.reshape(8, 8, 256)
        if h == 0:
            high, middle, _ = split3(massn[now].reshape(64, N))
            masses = dot(high, onehot_t[...], ((1,), (1,))) + dot(
                middle, onehot_t[...], ((1,), (1,))
            )
            rp[h][now, :, 0:8, HP:HP + 128] = masses.reshape(8, 8, 128)
            rp[h][now, :, 8:16, HP:HP + 128] = jnp.zeros((8, 8, 128), F32)

    def rs(h, k):
        if k < 12:
            kind, part = k // 2, PARTS[k % 2]
            src, dst = sb[h].at[kind, part], rb[h].at[kind, part]
            target = up2[h] if kind < 3 else down2[h]
        elif k < 18:
            src, dst = sb2[h].at[k - 12], rb2[h].at[k - 12]
            target = up1[h] if k < 15 else down1[h]
        else:
            src, dst, target = sb3[h], rb3[h], z_other
        return pltpu.make_async_remote_copy(
            src_ref=src, dst_ref=dst, send_sem=rs_send.at[h, k], recv_sem=rs_recv.at[h, k],
            device_id=target, device_id_type=MESH,
        )

    def put(h, kind, place, r, p, add=None):
        part = PARTS[p]
        rows = slice(r * 4 + part.start, r * 4 + part.stop)
        value = rp[h][place, rows]
        if add is not None:
            rs(h, 2 * add + p).wait_recv()
            value = value + rb[h][add, part].astype(F32)
        sb[h][kind, part] = value.astype(BF16)
        rs(h, 2 * kind + p).start()

    def insert_step(i, carry):
        @pl.when(i == 3)
        def _():
            for h in range(2):
                put(h, 2, 1, 0, 0, add=0)
                put(h, 5, 2, 1, 0, add=3)

        for h in range(2):
            insert_chunk(h, 3 - i)

            @pl.when(i == 0)
            def _():
                for p in range(2):
                    put(h, 0, 3, 0, p)
                    put(h, 3, 3, 1, p)

            @pl.when(i == 1)
            def _():
                put(h, 4, 2, 0, 0)

            @pl.when(i == 2)
            def _():
                put(h, 1, 1, 1, 0)

        return carry

    lax.fori_loop(0, 4, insert_step, 0)

    for h in range(2):
        put(h, 4, 2, 0, 1)
        put(h, 1, 1, 1, 1)
        put(h, 2, 1, 0, 1, add=0)
        put(h, 5, 2, 1, 1, add=3)

    def take(h, p):
        part = PARTS[p]
        for kind in (1, 2, 4, 5):
            rs(h, 2 * kind + p).wait_recv()
        for r, (from_below, from_above) in enumerate(((2, 4), (1, 5))):
            rows = slice(r * 4 + part.start, r * 4 + part.stop)
            rp[h][0, rows] = (
                rp[h][0, rows] + rb[h][from_below, part].astype(F32)
            ) + rb[h][from_above, part].astype(F32)

    def put_inner(h, kind, place, r, add=None):
        value = rp[h][0, r * 4 + place]
        if add is not None:
            rs(h, 12 + add).wait_recv()
            value = value + rb2[h][add].astype(F32)
        sb2[h][kind] = value.astype(BF16)
        rs(h, 12 + kind).start()

    for h in range(2):
        take(h, 0)
        put_inner(h, 0, 3, 0)
        put_inner(h, 3, 3, 1)
        put_inner(h, 1, 1, 1)
        put_inner(h, 4, 2, 0)
    for h in range(2):
        put_inner(h, 2, 1, 0, add=0)
        put_inner(h, 5, 2, 1, add=3)
    for h in range(2):
        take(h, 1)

    def own(h, r):
        from_below, from_above = ((2, 4), (1, 5))[r]
        return (
            rp[h][0, r * 4] + rb2[h][from_below].astype(F32)
        ) + rb2[h][from_above].astype(F32)

    for h in range(2):
        for k in (1, 2, 4, 5):
            rs(h, 12 + k).wait_recv()
        sb3[h][...] = own(h, 1).astype(BF16)
        rs(h, 18).start()

    for h in range(2):
        mine = own(h, 0)
        rs(h, 18).wait_recv()
        result = mine + rb3[h][...].astype(F32)
        sums_ref[:, h * HP:(h + 1) * HP] = result[0:8, 0:HP]
        sums_ref[:, PIX + h * HP:PIX + (h + 1) * HP] = result[8:16, 0:HP]
        if h == 0:
            weights_ref[...] = lax.dot_general(
                result[0:8, HP:HP + GROUPS], gain[...], (((1,), (0,)), ((), ())),
                precision=lax.Precision.HIGHEST, preferred_element_type=F32,
            )

    for h in range(2):
        for k in range(25):
            ag(h, k).wait_send()
        for k in range(19):
            rs(h, k).wait_send()
    for o in range(1, 8):
        dir_copy(o).wait_send()


def finish(sums_in, weights_in, stats_in, sums_ref, weights_ref, norm_ref, peak_ref):
    sums_ref[...] = sums_in[...]
    weights_ref[...] = weights_in[...]
    norm_ref[...] = stats_in[0:1]
    peak_ref[...] = stats_in[1:2]


def per_device(
    images, refs, ctf, noise_var, shifts, ctf_class, psi_prev, earlier_direction_range, view_range
):
    vmem = pl.BlockSpec(memory_space=pltpu.VMEM)
    hbm = pl.BlockSpec(memory_space=pl.ANY)
    smem = pl.BlockSpec(memory_space=pltpu.SMEM)
    wa, wb = WIDTHS
    dma = pltpu.SemaphoreType.DMA
    out = pl.pallas_call(
        kernel,
        out_shape=(
            jax.ShapeDtypeStruct((8, 2 * PIX), F32),
            jax.ShapeDtypeStruct((8, PIX), F32),
            jax.ShapeDtypeStruct((8, N), F32),
        ),
        in_specs=[hbm] * 8 + [smem, hbm],
        out_specs=(vmem, vmem, vmem),
        scratch_shapes=[
            pltpu.VMEM((N, 2 * PIX), BF16),
            pltpu.VMEM((8, 2 * PIX), BF16),
            pltpu.VMEM((GROUPS, PIX), F32),
            pltpu.VMEM((1, PIX), F32),
            pltpu.VMEM((8, N), jnp.int32),
            pltpu.VMEM((2, N), jnp.int32),
            pltpu.VMEM((16, PIX), F32),
            pltpu.VMEM((4, 2, 4, 16, HP), BF16),
            pltpu.VMEM((4, 2, 4, 16, HP), BF16),
            pltpu.VMEM((N, 2 * HP), BF16),
            pltpu.VMEM((N, 2 * HP), BF16),
            pltpu.VMEM((N, PIX), F32),
            pltpu.VMEM((6, N, 128), F32),
            pltpu.VMEM((OFFSETS * 64, 2 * HP), BF16),
            pltpu.VMEM((OFFSETS * 64, 2 * HP), BF16),
            pltpu.VMEM((64, HP), F32),
            pltpu.VMEM((GROUPS, PIX), F32),
            pltpu.VMEM((3, GROUPS, PIX), BF16),
            pltpu.VMEM((2, 4, 8, 8, 128), F32),
            pltpu.VMEM((128, N), BF16),
            pltpu.VMEM((2, 8, N), F32),
            pltpu.VMEM((2, 4, OFFSETS, 8, 8, N), F32),
            pltpu.VMEM((4, 8, 8, N), F32),
            pltpu.VMEM((OFFSETS, 4, 16, N), BF16),
            pltpu.VMEM((OFFSETS, 4, 16, N), BF16),
            pltpu.VMEM((4, 8, 16, wa), F32),
            pltpu.VMEM((4, 8, 16, wb), F32),
            pltpu.VMEM((8, 8, 128), F32),
            pltpu.VMEM((6, 4, 16, wa), BF16),
            pltpu.VMEM((6, 4, 16, wb), BF16),
            pltpu.VMEM((6, 4, 16, wa), BF16),
            pltpu.VMEM((6, 4, 16, wb), BF16),
            pltpu.VMEM((6, 16, wa), BF16),
            pltpu.VMEM((6, 16, wb), BF16),
            pltpu.VMEM((6, 16, wa), BF16),
            pltpu.VMEM((6, 16, wb), BF16),
            pltpu.VMEM((16, wa), BF16),
            pltpu.VMEM((16, wb), BF16),
            pltpu.VMEM((16, wa), BF16),
            pltpu.VMEM((16, wb), BF16),
            dma((9,)),
            dma((2, 25)),
            dma((2, 25)),
            dma((7,)),
            dma((7,)),
            dma((2, 19)),
            dma((2, 19)),
        ],
        compiler_params=pltpu.CompilerParams(
            collective_id=0, has_side_effects=True, vmem_limit_bytes=60 * 2**20
        ),
        cost_estimate=pl.CostEstimate(
            flops=10_000_000_000, bytes_accessed=4_000_000, transcendentals=600_000
        ),
        name="expectation_step",
    )(
        images, refs, ctf, noise_var.reshape(1, PIX), ctf_class.reshape(1, N),
        psi_prev.reshape(1, N), earlier_direction_range.reshape(1, N), shifts.T, view_range,
        jnp.asarray(phase_constants()),
    )
    class_sums, weight_sums, log_norm, peak_prob = pl.pallas_call(
        finish,
        out_shape=(
            jax.ShapeDtypeStruct((8, 2 * PIX), F32),
            jax.ShapeDtypeStruct((8, PIX), F32),
            jax.ShapeDtypeStruct((1, N), F32),
            jax.ShapeDtypeStruct((1, N), F32),
        ),
        in_specs=[vmem] * 3,
        out_specs=(vmem,) * 4,
        name="finish",
    )(*out)
    return class_sums, weight_sums, log_norm.reshape(N), peak_prob.reshape(N)


def solution(mesh):
    placed = (
        P("dom", None),
        P(("dir", "dom"), None),
        P(),
        P(),
        P("dom", None),
        P("dom"),
        P("dom"),
        P("dom"),
        P("dir"),
    )
    return jax.shard_map(
        per_device,
        mesh=mesh,
        in_specs=placed,
        out_specs=(P(("dir", "dom"), None), P(("dir", "dom"), None), P("dom"), P("dom")),
        check_vma=False,
    )
```

time: 76 us -> 63.2 us (0.83); the launches traced: 75.1 us -> 63 us
  local copies, waits for them, and re-layouts: 7.51 us -> 0 us
  Pallas kernels: 66.9 us -> 62.4 us
    pallas_call x1, Pallas kernels: 66.9 us -> 60.8 us  [per_device(): pl.pallas_call(kernel, out_shape=(jax.ShapeDtypeStruct((8, 2 * PIX), F32)...]
    unnamed x4 -> x0, local copies, waits for them, and re-layouts: 5.43 us -> none
    another operation x2 -> x0, local copies, waits for them, and re-layouts: 2.08 us -> none  [per_device(): jnp.stack([ctf_class, psi_prev, earlier_direction_range, shifts[:, 0], sh...]
    pallas_call x0 -> x1, Pallas kernels: none -> 1.63 us  [per_device(): pl.pallas_call(finish, out_shape=(jax.ShapeDtypeStruct((8, 2 * PIX), F32)...]
where the time goes in v2:
time: 63.2 us; the launch traced here: 63 us
  Pallas kernels  62.4 us (99%)
  between operations  0.64 us (1%)
    pallas_call x1, Pallas kernels, per_device(): pl.pallas_call(kernel, out_shape=(jax.ShapeDtypeStruct((8, 2 * PIX), F32)...  60.8 us
    pallas_call x1, Pallas kernels, per_device(): pl.pallas_call(finish, out_shape=(jax.ShapeDtypeStruct((8, 2 * PIX), F32)...  1.63 us

profile of v2, /device:TPU:2, one launch (start us, length us, event | category | flops | bytes accessed | tf_op | source)
XLA Modules:
  0.0 63.0 jit_solution(15670608906642062075)
XLA Ops:
  0.6 60.8 %expectation_step.1 = (f32[8,4096]{1,0:T(8,128)}, f32[8,2048]{1,0:T(8,128)}, f32[8,256]{1,0:T(8,128)}) custom-call(bf16[256,4096]{1,0:T(8,128)(2,1)} %images_ref.1, bf16[8,4096]{1,0:T(8,128)(2,1)} %refs_ref.1, f32[64,2048]{1,0:T(8,128)} %ctf_ref.1, f32[1,2048]{1,0:T(1,128)} %bitcast.7, s32[1,256]{1,0:T(1,128)} %bitcast.9, s32[1,256]{1,0:T(1,128)} %bitcast.10, ...), custom_call_target="tpu_custom_call" | custom-call | flops 10000000000 | bytes 4000000 | tf_op jit(solution)/shard_map/expectation_step/pallas_call | solution.py:640
  61.4 1.6 %finish.1 = (f32[8,4096]{1,0:T(8,128)}, f32[8,2048]{1,0:T(8,128)}, f32[1,256]{1,0:T(1,128)}, f32[1,256]{1,0:T(1,128)}) custom-call(f32[8,4096]{1,0:T(8,128)} %get-tuple-element.11.sums_in, f32[8,2048]{1,0:T(8,128)} %get-tuple-element.12.weights_in, f32[8,256]{1,0:T(8,128)} %get-tuple-element.13.stats_in), custom_call_target="tpu_custom_call" | custom-call | tf_op jit(solution)/shard_map/finish/pallas_call | solution.py:710

commit v3 on v2

--- a/solution.py
+++ b/solution.py
@@ -68,6 +68,13 @@
 
 def dot(a, b, dims):
     return lax.dot_general(a, b, (dims, ((), ())), preferred_element_type=F32)
+
+
+def tree(op, values):
+    while len(values) > 1:
+        pairs = [op(a, b) for a, b in zip(values[::2], values[1::2])]
+        values = pairs + values[len(pairs) * 2:]
+    return values[0]
 
 
 def ring(i):
@@ -117,9 +124,10 @@
 
     up2, down2 = (y_up, x_up), (y_down, x_down)
     up1, down1 = (x_up, y_up), (x_down, y_down)
+    far1 = (device(y, z, ring(x + 2)), device(ring(y + 2), z, x))
 
     barrier = pltpu.get_barrier_semaphore()
-    partners = [z_other, x_up, x_down, y_up, y_down] + dir_peers
+    partners = [z_other, x_up, x_down, y_up, y_down, *far1] + dir_peers
     for p in partners:
         pl.semaphore_signal(barrier, inc=1, device_id=p, device_id_type=MESH)
 
@@ -147,15 +155,9 @@
         if k == 0:
             src, dst, target = buf.at[0, 0, 0], buf.at[0, 1, 0], z_other
         elif k < 7:
-            kind = (k - 1) % 3
-            upward = k < 4
-            target = up1[h] if upward else down1[h]
-            side = 2 if upward else 1
-            if kind < 2:
-                src, dst = buf.at[0, kind, 0], buf.at[0, kind, side]
-            else:
-                r = 0 if upward else 1
-                src, dst = buf.at[0, r, side], buf.at[0, r, 3]
+            r, way = (k - 1) % 2, (k - 1) // 2
+            target = (up1, down1, far1)[way][h]
+            src, dst = buf.at[0, r, 0], buf.at[0, r, (2, 1, 3)[way]]
         else:
             piece = PIECES[(k - 7) % 3]
             kind = (k - 7) // 3
@@ -183,14 +185,14 @@
             for h in range(2):
                 ag(h, k).wait_recv()
 
-    Z_, UP, DOWN = 0, (1, 2, 3), (4, 5, 6)
+    Z_, INNER = 0, ((1, 3, 5), (2, 4, 6))
 
     def outer(kind, piece):
         return 7 + 3 * kind + piece
 
     U0, U1, UR, D0, D1, DR = range(6)
 
-    ag_start(Z_, UP[0], DOWN[0])
+    ag_start(Z_, *INNER[0])
     ag_start(outer(U0, 0), outer(D0, 0))
 
     for k in range(1, 7):
@@ -228,8 +230,11 @@
     psi_rows_sc[1] = psi_term[8:16]
 
     ag_wait(Z_)
-    ag_start(UP[1], DOWN[1])
+    ag_start(*INNER[1])
     ag_start(outer(U1, 0), outer(D1, 0))
+    ag_wait(*INNER[0])
+    for p in (1, 2):
+        ag_start(outer(U0, p), outer(D0, p))
 
     noise = noise_in[...]
     for j in range(8):
@@ -249,10 +254,8 @@
     loads[7].wait()
     loads[8].wait()
 
-    ag_wait(UP[0])
-    ag_start(UP[2])
-    ag_wait(DOWN[0])
-    ag_start(outer(U0, 1), outer(D0, 1))
+    ag_wait(outer(U0, 0))
+    ag_start(outer(UR, 0))
 
     def align(part, carry):
         rows = pl.ds(pl.multiple_of(part * 32, 32), 32)
@@ -283,19 +286,15 @@
         return carry
 
     lax.fori_loop(0, 4, align, 0)
-    ag_wait(outer(U0, 0))
-    ag_start(outer(UR, 0))
-    ag_wait(DOWN[1])
-    ag_start(DOWN[2])
-    ag_wait(UP[1])
-    ag_start(outer(D1, 1), outer(U1, 1))
+    ag_wait(*INNER[1])
+    for p in (1, 2):
+        ag_start(outer(D1, p), outer(U1, p))
     ag_wait(outer(D1, 0))
     ag_start(outer(DR, 0))
     lax.fori_loop(4, 8, align, 0)
-    ag_wait(UP[2])
-    ag_start(outer(U0, 2), outer(D0, 2))
-    ag_wait(DOWN[2])
-    ag_start(outer(D1, 2), outer(U1, 2))
+    for p in (1, 2):
+        ag_wait(outer(U0, p))
+        ag_start(outer(UR, p))
 
     def cross_chunk(h, now):
         for j in range(8):
@@ -332,14 +331,9 @@
     def cross_step(i, carry):
         @pl.when(i == 1)
         def _():
-            ag_wait(outer(U0, 1))
-            ag_start(outer(UR, 1))
-            ag_wait(outer(D1, 1))
-            ag_start(outer(DR, 1))
-            ag_wait(outer(U0, 2))
-            ag_start(outer(UR, 2))
-            ag_wait(outer(D1, 2))
-            ag_start(outer(DR, 2))
+            for p in (1, 2):
+                ag_wait(outer(D1, p))
+                ag_start(outer(DR, p))
             ag_wait(outer(D0, 0), outer(D0, 1), outer(D0, 2))
 
         @pl.when(i == 2)
@@ -353,6 +347,7 @@
 
         for h in range(2):
             cross_chunk(h, i)
+
         return carry
 
     lax.fori_loop(0, 4, cross_step, 0)
@@ -369,6 +364,7 @@
         ) + dot(low, picks, ((1,), (0,)))
         penalty = 0.5 * picked
         owner_y = ring(y + ahead_of(py))
+        tops = [top]
         for r in range(2):
             owner_z = lax.rem(z + r, 2)
             for px in range(4):
@@ -379,23 +375,28 @@
                 )
                 b = r * 4 + px
                 less = penalty[b * 8:(b + 1) * 8]
+                best_now = []
                 for t in range(OFFSETS):
                     value = sc[0, py, t, b] + sc[1, px, t, r * 4 + py]
                     value = (value - less) + prior
                     sc[0, py, t, b] = value
-                    top = jnp.maximum(top, value)
-        return top
+                    best_now.append(value)
+                tops.append(tree(jnp.maximum, best_now))
+        return tree(jnp.maximum, tops)
 
     top = lax.fori_loop(0, 4, score_pass, jnp.full((8, N), -jnp.inf, F32))
     top = jnp.max(top, axis=0, keepdims=True)
 
     def exp_pass(yy, total):
-        for t in range(OFFSETS):
-            for b in range(8):
+        sums = [total]
+        for b in range(8):
+            values = []
+            for t in range(OFFSETS):
                 value = jnp.exp(sc[0, yy, t, b] - top)
                 sc[0, yy, t, b] = value
-                total = total + value
-        return total
+                values.append(value)
+            sums.append(tree(jnp.add, values))
+        return tree(jnp.add, sums)
 
     total = lax.fori_loop(0, 4, exp_pass, jnp.zeros((8, N), F32))
     total = jnp.sum(total, axis=0, keepdims=True)
@@ -507,7 +508,7 @@
             target = up2[h] if kind < 3 else down2[h]
         elif k < 18:
             src, dst = sb2[h].at[k - 12], rb2[h].at[k - 12]
-            target = up1[h] if k < 15 else down1[h]
+            target = (far1, up1, down1)[(k - 12) % 3][h]
         else:
             src, dst, target = sb3[h], rb3[h], z_other
         return pltpu.make_async_remote_copy(
@@ -559,52 +560,39 @@
         put(h, 2, 1, 0, 1, add=0)
         put(h, 5, 2, 1, 1, add=3)
 
-    def take(h, p):
+    def take(h, p, r):
         part = PARTS[p]
-        for kind in (1, 2, 4, 5):
-            rs(h, 2 * kind + p).wait_recv()
-        for r, (from_below, from_above) in enumerate(((2, 4), (1, 5))):
-            rows = slice(r * 4 + part.start, r * 4 + part.stop)
-            rp[h][0, rows] = (
-                rp[h][0, rows] + rb[h][from_below, part].astype(F32)
-            ) + rb[h][from_above, part].astype(F32)
-
-    def put_inner(h, kind, place, r, add=None):
-        value = rp[h][0, r * 4 + place]
-        if add is not None:
-            rs(h, 12 + add).wait_recv()
-            value = value + rb2[h][add].astype(F32)
-        sb2[h][kind] = value.astype(BF16)
-        rs(h, 12 + kind).start()
+        from_below, from_above = ((2, 4), (1, 5))[r]
+        rs(h, 2 * from_below + p).wait_recv()
+        rs(h, 2 * from_above + p).wait_recv()
+        rows = slice(r * 4 + part.start, r * 4 + part.stop)
+        return (
+            rp[h][0, rows] + rb[h][from_below, part].astype(F32)
+        ) + rb[h][from_above, part].astype(F32)
+
+    for r in (1, 0):
+        for h in range(2):
+            above, below, far = (0, 1, 2)
+            taken = take(h, 0, r)
+            for k, place in enumerate((far, above, below)):
+                sb2[h][3 * r + k] = taken[place].astype(BF16)
+                rs(h, 12 + 3 * r + k).start()
+
+    def own(h, r):
+        total = take(h, 1, r)[0]
+        for k in range(3):
+            rs(h, 12 + 3 * r + k).wait_recv()
+            total = total + rb2[h][3 * r + k].astype(F32)
+        return total
 
     for h in range(2):
-        take(h, 0)
-        put_inner(h, 0, 3, 0)
-        put_inner(h, 3, 3, 1)
-        put_inner(h, 1, 1, 1)
-        put_inner(h, 4, 2, 0)
-    for h in range(2):
-        put_inner(h, 2, 1, 0, add=0)
-        put_inner(h, 5, 2, 1, add=3)
-    for h in range(2):
-        take(h, 1)
-
-    def own(h, r):
-        from_below, from_above = ((2, 4), (1, 5))[r]
-        return (
-            rp[h][0, r * 4] + rb2[h][from_below].astype(F32)
-        ) + rb2[h][from_above].astype(F32)
-
-    for h in range(2):
-        for k in (1, 2, 4, 5):
-            rs(h, 12 + k).wait_recv()
         sb3[h][...] = own(h, 1).astype(BF16)
         rs(h, 18).start()
+    mine = [own(h, 0) for h in range(2)]
 
     for h in range(2):
-        mine = own(h, 0)
         rs(h, 18).wait_recv()
-        result = mine + rb3[h][...].astype(F32)
+        result = mine[h] + rb3[h][...].astype(F32)
         sums_ref[:, h * HP:(h + 1) * HP] = result[0:8, 0:HP]
         sums_ref[:, PIX + h * HP:PIX + (h + 1) * HP] = result[8:16, 0:HP]
         if h == 0:

time: 63.2 us -> 59.2 us (0.937)
  Pallas kernels: 62.4 us -> 57.8 us
    pallas_call x1, Pallas kernels: 60.8 us -> 56.2 us  [per_device(): pl.pallas_call(kernel, out_shape=(jax.ShapeDtypeStruct((8, 2 * PIX), F32)...]
where the time goes in v3:
time: 59.2 us; the launch traced here: 58.5 us
  Pallas kernels  57.8 us (98%)
  between operations  0.64 us (1%)
    pallas_call x1, Pallas kernels, per_device(): pl.pallas_call(kernel, out_shape=(jax.ShapeDtypeStruct((8, 2 * PIX), F32)...  56.2 us
    pallas_call x1, Pallas kernels, per_device(): pl.pallas_call(finish, out_shape=(jax.ShapeDtypeStruct((8, 2 * PIX), F32)...  1.63 us

profile of v3, /device:TPU:2, one launch (start us, length us, event | category | flops | bytes accessed | tf_op | source)
XLA Modules:
  0.0 58.5 jit_solution(4563704385563136417)
XLA Ops:
  0.6 56.2 %expectation_step.1 = (f32[8,4096]{1,0:T(8,128)}, f32[8,2048]{1,0:T(8,128)}, f32[8,256]{1,0:T(8,128)}) custom-call(bf16[256,4096]{1,0:T(8,128)(2,1)} %images_ref.1, bf16[8,4096]{1,0:T(8,128)(2,1)} %refs_ref.1, f32[64,2048]{1,0:T(8,128)} %ctf_ref.1, f32[1,2048]{1,0:T(1,128)} %bitcast.7, s32[1,256]{1,0:T(1,128)} %bitcast.9, s32[1,256]{1,0:T(1,128)} %bitcast.10, ...), custom_call_target="tpu_custom_call" | custom-call | flops 10000000000 | bytes 4000000 | tf_op jit(solution)/shard_map/expectation_step/pallas_call | solution.py:628
  56.8 1.6 %finish.1 = (f32[8,4096]{1,0:T(8,128)}, f32[8,2048]{1,0:T(8,128)}, f32[1,256]{1,0:T(1,128)}, f32[1,256]{1,0:T(1,128)}) custom-call(f32[8,4096]{1,0:T(8,128)} %get-tuple-element.11.sums_in, f32[8,2048]{1,0:T(8,128)} %get-tuple-element.12.weights_in, f32[8,256]{1,0:T(8,128)} %get-tuple-element.13.stats_in), custom_call_target="tpu_custom_call" | custom-call | tf_op jit(solution)/shard_map/finish/pallas_call | solution.py:698

commit v4 on v3

--- a/solution.py
+++ b/solution.py
@@ -95,7 +95,7 @@
     sums_ref, weights_ref, stats_ref,
     img, refs_in, ctf, noise_in, ints, shift_in, table_ref,
     g_a, g_b, al_a, al_b, wsel, spin, s_a, s_b, mag, gain, gain3, en, onehot_t, psi_rows_sc,
-    sc, massn, l_a, l_b, rp_a, rp_b,
+    sc, massn, early, factor, l_a, l_b, rp_a, rp_b,
     st, sb_a, sb_b, rb_a, rb_b, sb2_a, sb2_b, rb2_a, rb2_b, sb3_a, sb3_b, rb3_a, rb3_b,
     load_sem, ag_send, ag_recv, dir_send, dir_recv, rs_send, rs_recv,
 ):
@@ -285,30 +285,21 @@
             ).astype(BF16)
         return carry
 
-    lax.fori_loop(0, 4, align, 0)
-    ag_wait(*INNER[1])
-    for p in (1, 2):
-        ag_start(outer(D1, p), outer(U1, p))
-    ag_wait(outer(D1, 0))
-    ag_start(outer(DR, 0))
-    lax.fori_loop(4, 8, align, 0)
-    for p in (1, 2):
-        ag_wait(outer(U0, p))
-        ag_start(outer(UR, p))
-
-    def cross_chunk(h, now):
+    lax.fori_loop(0, 8, align, 0)
+
+    def cross_chunk(h, now, r):
         for j in range(8):
             lanes = slice(j * 128, (j + 1) * 128)
             wide = slice(h * HP + j * 128, h * HP + (j + 1) * 128)
-            value = g[h][now, :, :, :, lanes].astype(F32).reshape(8, 16, 128)
+            value = g[h][now, r, :, :, lanes].astype(F32)
             real, imag = value[:, 0:8], value[:, 8:16]
-            mag[:, lanes] = (real * real + imag * imag).reshape(64, 128)
+            mag[:, lanes] = (real * real + imag * imag).reshape(32, 128)
 
             def put(t, shifted_real, shifted_imag):
-                rows = slice(t * 64, (t + 1) * 64)
-                s_buf[h][rows, lanes] = shifted_real.reshape(64, 128).astype(BF16)
+                rows = slice(t * 32, (t + 1) * 32)
+                s_buf[h][rows, lanes] = shifted_real.reshape(32, 128).astype(BF16)
                 s_buf[h][rows, HP + j * 128:HP + (j + 1) * 128] = (
-                    shifted_imag.reshape(64, 128).astype(BF16)
+                    shifted_imag.reshape(32, 128).astype(BF16)
                 )
 
             put(4, real, imag)
@@ -323,39 +314,19 @@
         by_high = dot(jnp.concatenate([high, middle, low], axis=0), gain3[0, :, half], ((1,), (1,)))
         by_middle = dot(jnp.concatenate([high, middle], axis=0), gain3[1, :, half], ((1,), (1,)))
         by_low = dot(high, gain3[2, :, half], ((1,), (1,)))
-        small = (by_low + by_high[128:192]) + by_middle[64:128]
-        energy = (small + (by_middle[0:64] + by_high[64:128])) + by_high[0:64]
-        en[h, now, :, :, 0:GROUPS] = energy.reshape(8, 8, GROUPS)
-        sc[h, now] = dot(s_buf[h][...], al[h][...], ((1,), (1,))).reshape(OFFSETS, 8, 8, N)
-
-    def cross_step(i, carry):
-        @pl.when(i == 1)
-        def _():
-            for p in (1, 2):
-                ag_wait(outer(D1, p))
-                ag_start(outer(DR, p))
-            ag_wait(outer(D0, 0), outer(D0, 1), outer(D0, 2))
-
-        @pl.when(i == 2)
-        def _():
-            ag_wait(outer(U1, 0), outer(U1, 1), outer(U1, 2))
-
-        @pl.when(i == 3)
-        def _():
-            for p in range(3):
-                ag_wait(outer(UR, p), outer(DR, p))
-
-        for h in range(2):
-            cross_chunk(h, i)
-
-        return carry
-
-    lax.fori_loop(0, 4, cross_step, 0)
-
-    def score_pass(py, top):
+        small = (by_low + by_high[64:96]) + by_middle[32:64]
+        energy = (small + (by_middle[0:32] + by_high[32:64])) + by_high[0:32]
+        blocks = pl.ds(r * 4, 4)
+        en[h, now, blocks, :, 0:GROUPS] = energy.reshape(4, 8, GROUPS)
+        sc[h, now, :, blocks] = dot(s_buf[h][...], al[h][...], ((1,), (1,))).reshape(
+            OFFSETS, 4, 8, N
+        )
+
+    def score_slab(py, places, top):
+        blocks = [(r, px) for r in range(2) for px in places]
         energies = [
             en[0, py, r * 4 + px, :, 0:GROUPS] + en[1, px, r * 4 + py, :, 0:GROUPS]
-            for r in range(2) for px in range(4)
+            for r, px in blocks
         ]
         high, middle, low = split3(jnp.concatenate(energies, axis=0))
         picks = onehot_t[0:GROUPS]
@@ -365,41 +336,130 @@
         penalty = 0.5 * picked
         owner_y = ring(y + ahead_of(py))
         tops = [top]
-        for r in range(2):
+        for k, (r, px) in enumerate(blocks):
             owner_z = lax.rem(z + r, 2)
-            for px in range(4):
-                owner_x = ring(x + (0, 1, 3, 2)[px])
-                view = views_ref[owner_y * 4 + owner_z * 2 + owner_x // 2]
-                prior = psi_rows_sc[lax.rem(owner_x, 2)] + jnp.where(
-                    ranges == view, F32(1.5), F32(0.0)
-                )
-                b = r * 4 + px
-                less = penalty[b * 8:(b + 1) * 8]
-                best_now = []
-                for t in range(OFFSETS):
-                    value = sc[0, py, t, b] + sc[1, px, t, r * 4 + py]
-                    value = (value - less) + prior
-                    sc[0, py, t, b] = value
-                    best_now.append(value)
-                tops.append(tree(jnp.maximum, best_now))
-        return tree(jnp.maximum, tops)
-
-    top = lax.fori_loop(0, 4, score_pass, jnp.full((8, N), -jnp.inf, F32))
-    top = jnp.max(top, axis=0, keepdims=True)
-
-    def exp_pass(yy, total):
-        sums = [total]
-        for b in range(8):
+            owner_x = ring(x + (0, 1, 3, 2)[px])
+            view = views_ref[owner_y * 4 + owner_z * 2 + owner_x // 2]
+            prior = psi_rows_sc[lax.rem(owner_x, 2)] + jnp.where(
+                ranges == view, F32(1.5), F32(0.0)
+            )
+            less = penalty[k * 8:(k + 1) * 8]
             values = []
             for t in range(OFFSETS):
-                value = jnp.exp(sc[0, yy, t, b] - top)
-                sc[0, yy, t, b] = value
+                value = sc[0, py, t, r * 4 + px] + sc[1, px, t, r * 4 + py]
+                value = (value - less) + prior
+                sc[0, py, t, r * 4 + px] = value
                 values.append(value)
-            sums.append(tree(jnp.add, values))
+            tops.append(tree(jnp.maximum, values))
+        return tree(jnp.maximum, tops)
+
+    def combine(py, b, e):
+        by_row = []
+        for ty in range(3):
+            minus, zero, plus = e[3 * ty], e[3 * ty + 1], e[3 * ty + 2]
+            by_row.append((zero, plus + minus, plus - minus))
+        out = []
+        for k in range(3):
+            minus, zero, plus = by_row[0][k], by_row[1][k], by_row[2][k]
+            out.append((zero, plus + minus, plus - minus))
+        order = (
+            out[0][0], out[1][0], out[0][1], out[1][1], out[2][2],
+            out[2][0], out[2][1], out[0][2], out[1][2],
+        )
+        for k in range(OFFSETS):
+            sc[1, py, k, b] = order[k]
+        massn[py, b] = (out[0][0] + out[1][0]) + (out[0][1] + out[1][1])
+
+    def exp_slab(py, places, top, total, combined):
+        sums = [total]
+        for r in range(2):
+            for px in places:
+                b = r * 4 + px
+                values = []
+                for t in range(OFFSETS):
+                    value = jnp.exp(sc[0, py, t, b] - top)
+                    if not combined:
+                        sc[0, py, t, b] = value
+                    values.append(value)
+                sums.append(tree(jnp.add, values))
+                if combined:
+                    combine(py, b, values)
         return tree(jnp.add, sums)
 
-    total = lax.fori_loop(0, 4, exp_pass, jnp.zeros((8, N), F32))
-    total = jnp.sum(total, axis=0, keepdims=True)
+    def combine_slab(py, places):
+        for r in range(2):
+            for px in places:
+                b = r * 4 + px
+                combine(py, b, [sc[0, py, t, b] for t in range(OFFSETS)])
+
+    nearby, every, lowest = (0, 1, 2), (0, 1, 2, 3), jnp.full((8, N), -jnp.inf, F32)
+    nothing = jnp.zeros((8, N), F32)
+
+    def early_scores():
+        top = lax.fori_loop(0, 3, lambda py, v: score_slab(py, nearby, v), lowest)
+        top = jnp.max(top, axis=0, keepdims=True)
+        total = lax.fori_loop(
+            0, 3, lambda py, v: exp_slab(py, nearby, top, v, True), nothing
+        )
+        early[0:1] = top
+        early[1:2] = jnp.sum(total, axis=0, keepdims=True)
+
+    def relay(arrived, onward, *ps):
+        for p in ps:
+            ag_wait(outer(arrived, p))
+            ag_start(outer(onward, p))
+
+    def cross_step(i, carry):
+        @pl.when(i == 1)
+        def _():
+            ag_wait(*INNER[1])
+            for p in (1, 2):
+                ag_start(outer(D1, p), outer(U1, p))
+
+        @pl.when(i == 2)
+        def _():
+            relay(U0, UR, 1, 2)
+            relay(D1, DR, 0)
+            ag_wait(outer(D0, 0), outer(D0, 1), outer(D0, 2))
+
+        @pl.when(i == 4)
+        def _():
+            relay(D1, DR, 1, 2)
+
+        @pl.when(i == 5)
+        def _():
+            ag_wait(outer(U1, 0), outer(U1, 1), outer(U1, 2))
+
+        @pl.when(i == 6)
+        def _():
+            early_scores()
+            ag_wait(outer(UR, 0), outer(UR, 1), outer(UR, 2))
+
+        @pl.when(i == 7)
+        def _():
+            ag_wait(outer(DR, 0), outer(DR, 1), outer(DR, 2))
+
+        u, v = i // 2, lax.rem(i, 2)
+        sides = (u * (3 - u)) // 2
+        now = sides * (1 + v) + (1 - sides) * u
+        r = sides * (u - 1) + (1 - sides) * v
+        for h in range(2):
+            cross_chunk(h, now, r)
+        return carry
+
+    lax.fori_loop(0, 8, cross_step, 0)
+
+    late_top = lax.fori_loop(0, 3, lambda py, v: score_slab(py, (3,), v), lowest)
+    late_top = jnp.max(score_slab(3, every, late_top), axis=0, keepdims=True)
+    late_total = lax.fori_loop(
+        0, 3, lambda py, v: exp_slab(py, (3,), late_top, v, False), nothing
+    )
+    late_total = jnp.sum(
+        exp_slab(3, every, late_top, late_total, False), axis=0, keepdims=True
+    )
+    early_top = early[0:1]
+    top = jnp.maximum(early_top, late_top)
+    total = early[1:2] * jnp.exp(early_top - top) + late_total * jnp.exp(late_top - top)
 
     for half in range(2):
         lanes = slice(half * 128, (half + 1) * 128)
@@ -421,6 +481,14 @@
 
     for o in range(1, 8):
         dir_copy(o).start()
+
+    def combine_late(py, carry):
+        combine_slab(py, (3,))
+        return carry
+
+    lax.fori_loop(0, 3, combine_late, 0)
+    combine_slab(3, every)
+
     for o in range(1, 8):
         dir_arrival(o).wait_recv()
 
@@ -437,42 +505,20 @@
     log_norm = best + jnp.log(mass_all)
     stats_ref[0:1] = log_norm
     stats_ref[1:2] = jnp.exp(best - log_norm)
-    factor = jnp.exp(top - log_norm)
-
-    def posterior_pass(yy, carry):
-        for b in range(8):
-            p = [
-                (sc[0, yy, t, b] * factor).astype(BF16).astype(F32) for t in range(OFFSETS)
-            ]
-            by_row = []
-            for ty in range(3):
-                minus, zero, plus = p[3 * ty], p[3 * ty + 1], p[3 * ty + 2]
-                by_row.append((zero, plus + minus, plus - minus))
-            out = []
-            for k in range(3):
-                minus, zero, plus = by_row[0][k], by_row[1][k], by_row[2][k]
-                out.append((zero, plus + minus, plus - minus))
-            order = (
-                out[0][0], out[1][0], out[0][1], out[1][1], out[2][2],
-                out[2][0], out[2][1], out[0][2], out[1][2],
-            )
-            for k in range(OFFSETS):
-                sc[1, yy, k, b] = order[k]
-            massn[yy, b] = (out[0][0] + out[1][0]) + (out[0][1] + out[1][1])
-        return carry
-
-    lax.fori_loop(0, 4, posterior_pass, 0)
+    factor[0] = jnp.broadcast_to(jnp.exp(early_top - log_norm), (8, N))
+    factor[1] = jnp.broadcast_to(jnp.exp(late_top - log_norm), (8, N))
 
     def insert_chunk(h, now):
+        scale = [factor[now // 3]] * 3 + [factor[1]]
         for zz in range(2):
             for cp in range(2):
                 pair = []
                 for c in range(2):
                     cc = 2 * cp + c
                     if h == 0:
-                        pair.append(sc[1, now, :, zz * 4 + cc])
+                        pair.append(sc[1, now, :, zz * 4 + cc] * scale[cc])
                     else:
-                        pair.append(sc[1, cc, :, zz * 4 + now])
+                        pair.append(sc[1, cc, :, zz * 4 + now] * scale[cc])
                 l_buf[h][:, zz * 2 + cp] = jnp.concatenate(pair, axis=1).astype(BF16)
         left = l_buf[h][...].reshape(OFFSETS * 64, N)
         for q in range(4):
@@ -494,7 +540,8 @@
             rp[h][now, :, 0:8, lanes] = total_real.reshape(8, 8, 256)
             rp[h][now, :, 8:16, lanes] = total_imag.reshape(8, 8, 256)
         if h == 0:
-            high, middle, _ = split3(massn[now].reshape(64, N))
+            weighted = [massn[now, b] * scale[b % 4] for b in range(8)]
+            high, middle, _ = split3(jnp.concatenate(weighted, axis=0))
             masses = dot(high, onehot_t[...], ((1,), (1,))) + dot(
                 middle, onehot_t[...], ((1,), (1,))
             )
@@ -648,9 +695,9 @@
             pltpu.VMEM((N, 2 * HP), BF16),
             pltpu.VMEM((N, PIX), F32),
             pltpu.VMEM((6, N, 128), F32),
-            pltpu.VMEM((OFFSETS * 64, 2 * HP), BF16),
-            pltpu.VMEM((OFFSETS * 64, 2 * HP), BF16),
-            pltpu.VMEM((64, HP), F32),
+            pltpu.VMEM((OFFSETS * 32, 2 * HP), BF16),
+            pltpu.VMEM((OFFSETS * 32, 2 * HP), BF16),
+            pltpu.VMEM((32, HP), F32),
             pltpu.VMEM((GROUPS, PIX), F32),
             pltpu.VMEM((3, GROUPS, PIX), BF16),
             pltpu.VMEM((2, 4, 8, 8, 128), F32),
@@ -658,6 +705,8 @@
             pltpu.VMEM((2, 8, N), F32),
             pltpu.VMEM((2, 4, OFFSETS, 8, 8, N), F32),
             pltpu.VMEM((4, 8, 8, N), F32),
+            pltpu.VMEM((8, N), F32),
+            pltpu.VMEM((2, 8, N), F32),
             pltpu.VMEM((OFFSETS, 4, 16, N), BF16),
             pltpu.VMEM((OFFSETS, 4, 16, N), BF16),
             pltpu.VMEM((4, 8, 16, wa), F32),

time: 59.2 us -> 58.1 us (0.981)
  Pallas kernels: 57.8 us -> 56.7 us
    pallas_call x1, Pallas kernels: 56.2 us -> 55.1 us  [per_device(): pl.pallas_call(kernel, out_shape=(jax.ShapeDtypeStruct((8, 2 * PIX), F32)...]
where the time goes in v4:
time: 58.1 us; the launch traced here: 57.3 us
  Pallas kernels  56.7 us (98%)
  between operations  0.64 us (1%)
    pallas_call x1, Pallas kernels, per_device(): pl.pallas_call(kernel, out_shape=(jax.ShapeDtypeStruct((8, 2 * PIX), F32)...  55.1 us
    pallas_call x1, Pallas kernels, per_device(): pl.pallas_call(finish, out_shape=(jax.ShapeDtypeStruct((8, 2 * PIX), F32)...  1.63 us

profile of v4, /device:TPU:2, one launch (start us, length us, event | category | flops | bytes accessed | tf_op | source)
XLA Modules:
  0.0 57.3 jit_solution(9013082986038142326)
XLA Ops:
  0.6 55.1 %expectation_step.1 = (f32[8,4096]{1,0:T(8,128)}, f32[8,2048]{1,0:T(8,128)}, f32[8,256]{1,0:T(8,128)}) custom-call(bf16[256,4096]{1,0:T(8,128)(2,1)} %images_ref.1, bf16[8,4096]{1,0:T(8,128)(2,1)} %refs_ref.1, f32[64,2048]{1,0:T(8,128)} %ctf_ref.1, f32[1,2048]{1,0:T(1,128)} %bitcast.7, s32[1,256]{1,0:T(1,128)} %bitcast.9, s32[1,256]{1,0:T(1,128)} %bitcast.10, ...), custom_call_target="tpu_custom_call" | custom-call | flops 10000000000 | bytes 4000000 | tf_op jit(solution)/shard_map/expectation_step/pallas_call | solution.py:675
  55.7 1.6 %finish.1 = (f32[8,4096]{1,0:T(8,128)}, f32[8,2048]{1,0:T(8,128)}, f32[1,256]{1,0:T(1,128)}, f32[1,256]{1,0:T(1,128)}) custom-call(f32[8,4096]{1,0:T(8,128)} %get-tuple-element.11.sums_in, f32[8,2048]{1,0:T(8,128)} %get-tuple-element.12.weights_in, f32[8,256]{1,0:T(8,128)} %get-tuple-element.13.stats_in), custom_call_target="tpu_custom_call" | custom-call | tf_op jit(solution)/shard_map/finish/pallas_call | solution.py:747

commit v5 on v4

--- a/solution.py
+++ b/solution.py
@@ -91,9 +91,9 @@
 
 def kernel(
     images_ref, refs_ref, ctf_ref, noise_ref, class_ref, psi_ref, range_ref, shift_ref,
-    views_ref, table_in,
+    views_in, table_in,
     sums_ref, weights_ref, stats_ref,
-    img, refs_in, ctf, noise_in, ints, shift_in, table_ref,
+    views_ref, img, refs_in, ctf, noise_in, ints, shift_in, table_ref,
     g_a, g_b, al_a, al_b, wsel, spin, s_a, s_b, mag, gain, gain3, en, onehot_t, psi_rows_sc,
     sc, massn, early, factor, l_a, l_b, rp_a, rp_b,
     st, sb_a, sb_b, rb_a, rb_b, sb2_a, sb2_b, rb2_a, rb2_b, sb3_a, sb3_b, rb3_a, rb3_b,
@@ -137,6 +137,7 @@
             (refs_ref, refs_in), (shift_ref, shift_in), (class_ref, ints.at[0:1]),
             (psi_ref, ints.at[1:2]), (range_ref, ints.at[2:3]), (noise_ref, noise_in),
             (ctf_ref, ctf), (images_ref, img), (table_in, table_ref),
+            (views_in, views_ref),
         ))
     ]
     for load in loads:
@@ -253,6 +254,7 @@
 
     loads[7].wait()
     loads[8].wait()
+    loads[9].wait()
 
     ag_wait(outer(U0, 0))
     ag_start(outer(UR, 0))
@@ -479,7 +481,7 @@
             recv_sem=dir_recv.at[o - 1], device_id=dir_peers[o - 1], device_id_type=MESH,
         )
 
-    for o in range(1, 8):
+    for o in (4, 5, 3, 2, 6, 7, 1):
         dir_copy(o).start()
 
     def combine_late(py, carry):
@@ -488,6 +490,9 @@
 
     lax.fori_loop(0, 3, combine_late, 0)
     combine_slab(3, every)
+    for h in range(2):
+        for k in range(25):
+            ag(h, k).wait_send()
 
     for o in range(1, 8):
         dir_arrival(o).wait_recv()
@@ -638,6 +643,12 @@
     mine = [own(h, 0) for h in range(2)]
 
     for h in range(2):
+        for k in range(18):
+            rs(h, k).wait_send()
+    for o in range(1, 8):
+        dir_copy(o).wait_send()
+
+    for h in range(2):
         rs(h, 18).wait_recv()
         result = mine[h] + rb3[h][...].astype(F32)
         sums_ref[:, h * HP:(h + 1) * HP] = result[0:8, 0:HP]
@@ -649,12 +660,7 @@
             )
 
     for h in range(2):
-        for k in range(25):
-            ag(h, k).wait_send()
-        for k in range(19):
-            rs(h, k).wait_send()
-    for o in range(1, 8):
-        dir_copy(o).wait_send()
+        rs(h, 18).wait_send()
 
 
 def finish(sums_in, weights_in, stats_in, sums_ref, weights_ref, norm_ref, peak_ref):
@@ -669,7 +675,6 @@
 ):
     vmem = pl.BlockSpec(memory_space=pltpu.VMEM)
     hbm = pl.BlockSpec(memory_space=pl.ANY)
-    smem = pl.BlockSpec(memory_space=pltpu.SMEM)
     wa, wb = WIDTHS
     dma = pltpu.SemaphoreType.DMA
     out = pl.pallas_call(
@@ -679,9 +684,10 @@
             jax.ShapeDtypeStruct((8, PIX), F32),
             jax.ShapeDtypeStruct((8, N), F32),
         ),
-        in_specs=[hbm] * 8 + [smem, hbm],
+        in_specs=[hbm] * 10,
         out_specs=(vmem, vmem, vmem),
         scratch_shapes=[
+            pltpu.SMEM((16,), jnp.int32),
             pltpu.VMEM((N, 2 * PIX), BF16),
             pltpu.VMEM((8, 2 * PIX), BF16),
             pltpu.VMEM((GROUPS, PIX), F32),
@@ -724,7 +730,7 @@
             pltpu.VMEM((16, wb), BF16),
             pltpu.VMEM((16, wa), BF16),
             pltpu.VMEM((16, wb), BF16),
-            dma((9,)),
+            dma((10,)),
             dma((2, 25)),
             dma((2, 25)),
             dma((7,)),

time: 58.1 us -> 57.2 us (0.985)
  Pallas kernels: 56.7 us -> 55.9 us
    pallas_call x1, Pallas kernels: 55.1 us -> 54.2 us  [per_device(): pl.pallas_call(kernel, out_shape=(jax.ShapeDtypeStruct((8, 2 * PIX), F32)...]
where the time goes in v5:
time: 57.2 us; the launch traced here: 56.5 us
  Pallas kernels  55.9 us (98%)
  between operations  0.64 us (1%)
    pallas_call x1, Pallas kernels, per_device(): pl.pallas_call(kernel, out_shape=(jax.ShapeDtypeStruct((8, 2 * PIX), F32)...  54.2 us
    pallas_call x1, Pallas kernels, per_device(): pl.pallas_call(finish, out_shape=(jax.ShapeDtypeStruct((8, 2 * PIX), F32)...  1.63 us

profile of v5, /device:TPU:2, one launch (start us, length us, event | category | flops | bytes accessed | tf_op | source)
XLA Modules:
  0.0 56.5 jit_solution(10107452226582700820)
XLA Ops:
  0.6 54.2 %expectation_step.1 = (f32[8,4096]{1,0:T(8,128)}, f32[8,2048]{1,0:T(8,128)}, f32[8,256]{1,0:T(8,128)}) custom-call(bf16[256,4096]{1,0:T(8,128)(2,1)} %images_ref.1, bf16[8,4096]{1,0:T(8,128)(2,1)} %refs_ref.1, f32[64,2048]{1,0:T(8,128)} %ctf_ref.1, f32[1,2048]{1,0:T(1,128)} %bitcast.7, s32[1,256]{1,0:T(1,128)} %bitcast.9, s32[1,256]{1,0:T(1,128)} %bitcast.10, ...), custom_call_target="tpu_custom_call" | custom-call | flops 10000000000 | bytes 4000000 | tf_op jit(solution)/shard_map/expectation_step/pallas_call | solution.py:680
  54.9 1.6 %finish.1 = (f32[8,4096]{1,0:T(8,128)}, f32[8,2048]{1,0:T(8,128)}, f32[1,256]{1,0:T(1,128)}, f32[1,256]{1,0:T(1,128)}) custom-call(f32[8,4096]{1,0:T(8,128)} %get-tuple-element.11.sums_in, f32[8,2048]{1,0:T(8,128)} %get-tuple-element.12.weights_in, f32[8,256]{1,0:T(8,128)} %get-tuple-element.13.stats_in), custom_call_target="tpu_custom_call" | custom-call | tf_op jit(solution)/shard_map/finish/pallas_call | solution.py:753

commit v6 on v5

--- a/solution.py
+++ b/solution.py
@@ -289,19 +289,22 @@
 
     lax.fori_loop(0, 8, align, 0)
 
-    def cross_chunk(h, now, r):
+    def cross_chunk(h, slabs, r):
+        many = 32 * len(slabs)
         for j in range(8):
             lanes = slice(j * 128, (j + 1) * 128)
             wide = slice(h * HP + j * 128, h * HP + (j + 1) * 128)
-            value = g[h][now, r, :, :, lanes].astype(F32)
+            value = jnp.concatenate(
+                [g[h][now, r, :, :, lanes].astype(F32) for now in slabs], axis=0
+            )
             real, imag = value[:, 0:8], value[:, 8:16]
-            mag[:, lanes] = (real * real + imag * imag).reshape(32, 128)
+            mag[0:many, lanes] = (real * real + imag * imag).reshape(many, 128)
 
             def put(t, shifted_real, shifted_imag):
-                rows = slice(t * 32, (t + 1) * 32)
-                s_buf[h][rows, lanes] = shifted_real.reshape(32, 128).astype(BF16)
+                rows = slice(t * many, (t + 1) * many)
+                s_buf[h][rows, lanes] = shifted_real.reshape(many, 128).astype(BF16)
                 s_buf[h][rows, HP + j * 128:HP + (j + 1) * 128] = (
-                    shifted_imag.reshape(32, 128).astype(BF16)
+                    shifted_imag.reshape(many, 128).astype(BF16)
                 )
 
             put(4, real, imag)
@@ -311,18 +314,21 @@
                 rc_, is_, rs_, ic_ = real * c, imag * s, real * s, imag * c
                 put(offset_index(ty, tx), rc_ - is_, rs_ + ic_)
                 put(offset_index(-ty, -tx), rc_ + is_, ic_ - rs_)
-        high, middle, low = split3(mag[...])
+        high, middle, low = split3(mag[0:many])
         half = slice(h * HP, (h + 1) * HP)
         by_high = dot(jnp.concatenate([high, middle, low], axis=0), gain3[0, :, half], ((1,), (1,)))
         by_middle = dot(jnp.concatenate([high, middle], axis=0), gain3[1, :, half], ((1,), (1,)))
         by_low = dot(high, gain3[2, :, half], ((1,), (1,)))
-        small = (by_low + by_high[64:96]) + by_middle[32:64]
-        energy = (small + (by_middle[0:32] + by_high[32:64])) + by_high[0:32]
+        small = (by_low + by_high[2 * many:]) + by_middle[many:]
+        energy = (small + (by_middle[0:many] + by_high[many:2 * many])) + by_high[0:many]
+        energy = energy.reshape(len(slabs), 4, 8, GROUPS)
+        cross = dot(s_buf[h][0:OFFSETS * many], al[h][...], ((1,), (1,))).reshape(
+            OFFSETS, len(slabs), 4, 8, N
+        )
         blocks = pl.ds(r * 4, 4)
-        en[h, now, blocks, :, 0:GROUPS] = energy.reshape(4, 8, GROUPS)
-        sc[h, now, :, blocks] = dot(s_buf[h][...], al[h][...], ((1,), (1,))).reshape(
-            OFFSETS, 4, 8, N
-        )
+        for k, now in enumerate(slabs):
+            en[h, now, blocks, :, 0:GROUPS] = energy[k]
+            sc[h, now, :, blocks] = cross[:, k]
 
     def score_slab(py, places, top):
         blocks = [(r, px) for r in range(2) for px in places]
@@ -411,45 +417,50 @@
             ag_wait(outer(arrived, p))
             ag_start(outer(onward, p))
 
-    def cross_step(i, carry):
-        @pl.when(i == 1)
+    def own_step(r, carry):
+        @pl.when(r == 1)
         def _():
             ag_wait(*INNER[1])
             for p in (1, 2):
                 ag_start(outer(D1, p), outer(U1, p))
 
-        @pl.when(i == 2)
+        for h in range(2):
+            cross_chunk(h, (0,), r)
+        return carry
+
+    def sides_step(r, carry):
+        @pl.when(r == 0)
         def _():
             relay(U0, UR, 1, 2)
             relay(D1, DR, 0)
             ag_wait(outer(D0, 0), outer(D0, 1), outer(D0, 2))
 
-        @pl.when(i == 4)
+        @pl.when(r == 1)
         def _():
             relay(D1, DR, 1, 2)
-
-        @pl.when(i == 5)
-        def _():
             ag_wait(outer(U1, 0), outer(U1, 1), outer(U1, 2))
 
-        @pl.when(i == 6)
+        for h in range(2):
+            cross_chunk(h, (1, 2), r)
+        return carry
+
+    def far_step(r, carry):
+        @pl.when(r == 0)
         def _():
             early_scores()
             ag_wait(outer(UR, 0), outer(UR, 1), outer(UR, 2))
 
-        @pl.when(i == 7)
+        @pl.when(r == 1)
         def _():
             ag_wait(outer(DR, 0), outer(DR, 1), outer(DR, 2))
 
-        u, v = i // 2, lax.rem(i, 2)
-        sides = (u * (3 - u)) // 2
-        now = sides * (1 + v) + (1 - sides) * u
-        r = sides * (u - 1) + (1 - sides) * v
         for h in range(2):
-            cross_chunk(h, now, r)
+            cross_chunk(h, (3,), r)
         return carry
 
-    lax.fori_loop(0, 8, cross_step, 0)
+    lax.fori_loop(0, 2, own_step, 0)
+    lax.fori_loop(0, 2, sides_step, 0)
+    lax.fori_loop(0, 2, far_step, 0)
 
     late_top = lax.fori_loop(0, 3, lambda py, v: score_slab(py, (3,), v), lowest)
     late_top = jnp.max(score_slab(3, every, late_top), axis=0, keepdims=True)
@@ -701,9 +712,9 @@
             pltpu.VMEM((N, 2 * HP), BF16),
             pltpu.VMEM((N, PIX), F32),
             pltpu.VMEM((6, N, 128), F32),
-            pltpu.VMEM((OFFSETS * 32, 2 * HP), BF16),
-            pltpu.VMEM((OFFSETS * 32, 2 * HP), BF16),
-            pltpu.VMEM((32, HP), F32),
+            pltpu.VMEM((OFFSETS * 64, 2 * HP), BF16),
+            pltpu.VMEM((OFFSETS * 64, 2 * HP), BF16),
+            pltpu.VMEM((64, HP), F32),
             pltpu.VMEM((GROUPS, PIX), F32),
             pltpu.VMEM((3, GROUPS, PIX), BF16),
             pltpu.VMEM((2, 4, 8, 8, 128), F32),

time: 57.2 us -> 56.8 us (level)
  no operation moved by 1% of the time
where the time goes in v6:
time: 56.8 us; the launch traced here: 56.5 us
  Pallas kernels  55.8 us (98%)
  between operations  0.64 us (1%)
    pallas_call x1, Pallas kernels, per_device(): pl.pallas_call(kernel, out_shape=(jax.ShapeDtypeStruct((8, 2 * PIX), F32)...  54.2 us
    pallas_call x1, Pallas kernels, per_device(): pl.pallas_call(finish, out_shape=(jax.ShapeDtypeStruct((8, 2 * PIX), F32)...  1.63 us

profile of v6, /device:TPU:2, one launch (start us, length us, event | category | flops | bytes accessed | tf_op | source)
XLA Modules:
  0.0 56.5 jit_solution(9591771550427513049)
XLA Ops:
  0.6 54.2 %expectation_step.1 = (f32[8,4096]{1,0:T(8,128)}, f32[8,2048]{1,0:T(8,128)}, f32[8,256]{1,0:T(8,128)}) custom-call(bf16[256,4096]{1,0:T(8,128)(2,1)} %images_ref.1, bf16[8,4096]{1,0:T(8,128)(2,1)} %refs_ref.1, f32[64,2048]{1,0:T(8,128)} %ctf_ref.1, f32[1,2048]{1,0:T(1,128)} %bitcast.7, s32[1,256]{1,0:T(1,128)} %bitcast.9, s32[1,256]{1,0:T(1,128)} %bitcast.10, ...), custom_call_target="tpu_custom_call" | custom-call | flops 10000000000 | bytes 4000000 | tf_op jit(solution)/shard_map/expectation_step/pallas_call | solution.py:691
  54.8 1.6 %finish.1 = (f32[8,4096]{1,0:T(8,128)}, f32[8,2048]{1,0:T(8,128)}, f32[1,256]{1,0:T(1,128)}, f32[1,256]{1,0:T(1,128)}) custom-call(f32[8,4096]{1,0:T(8,128)} %get-tuple-element.11.sums_in, f32[8,2048]{1,0:T(8,128)} %get-tuple-element.12.weights_in, f32[8,256]{1,0:T(8,128)} %get-tuple-element.13.stats_in), custom_call_target="tpu_custom_call" | custom-call | tf_op jit(solution)/shard_map/finish/pallas_call | solution.py:764

commit v7 on v6

--- a/solution.py
+++ b/solution.py
@@ -593,8 +593,9 @@
         @pl.when(i == 3)
         def _():
             for h in range(2):
+                put(h, 5, 2, 1, 0, add=3)
+            for h in range(2):
                 put(h, 2, 1, 0, 0, add=0)
-                put(h, 5, 2, 1, 0, add=3)
 
         for h in range(2):
             insert_chunk(h, 3 - i)
@@ -618,10 +619,11 @@
     lax.fori_loop(0, 4, insert_step, 0)
 
     for h in range(2):
+        put(h, 1, 1, 1, 1)
+        put(h, 5, 2, 1, 1, add=3)
+    for h in range(2):
         put(h, 4, 2, 0, 1)
-        put(h, 1, 1, 1, 1)
         put(h, 2, 1, 0, 1, add=0)
-        put(h, 5, 2, 1, 1, add=3)
 
     def take(h, p, r):
         part = PARTS[p]

time: 56.8 us -> 56.8 us (level)
  no operation moved by 1% of the time
where the time goes in v7:
time: 56.8 us; the launch traced here: 56.5 us
  Pallas kernels  55.8 us (98%)
  between operations  0.64 us (1%)
    pallas_call x1, Pallas kernels, per_device(): pl.pallas_call(kernel, out_shape=(jax.ShapeDtypeStruct((8, 2 * PIX), F32)...  54.2 us
    pallas_call x1, Pallas kernels, per_device(): pl.pallas_call(finish, out_shape=(jax.ShapeDtypeStruct((8, 2 * PIX), F32)...  1.63 us

profile of v7, /device:TPU:2, one launch (start us, length us, event | category | flops | bytes accessed | tf_op | source)
XLA Modules:
  0.0 56.5 jit_solution(9736883602996484883)
XLA Ops:
  0.6 54.2 %expectation_step.1 = (f32[8,4096]{1,0:T(8,128)}, f32[8,2048]{1,0:T(8,128)}, f32[8,256]{1,0:T(8,128)}) custom-call(bf16[256,4096]{1,0:T(8,128)(2,1)} %images_ref.1, bf16[8,4096]{1,0:T(8,128)(2,1)} %refs_ref.1, f32[64,2048]{1,0:T(8,128)} %ctf_ref.1, f32[1,2048]{1,0:T(1,128)} %bitcast.7, s32[1,256]{1,0:T(1,128)} %bitcast.9, s32[1,256]{1,0:T(1,128)} %bitcast.10, ...), custom_call_target="tpu_custom_call" | custom-call | flops 10000000000 | bytes 4000000 | tf_op jit(solution)/shard_map/expectation_step/pallas_call | solution.py:693
  54.8 1.6 %finish.1 = (f32[8,4096]{1,0:T(8,128)}, f32[8,2048]{1,0:T(8,128)}, f32[1,256]{1,0:T(1,128)}, f32[1,256]{1,0:T(1,128)}) custom-call(f32[8,4096]{1,0:T(8,128)} %get-tuple-element.11.sums_in, f32[8,2048]{1,0:T(8,128)} %get-tuple-element.12.weights_in, f32[8,256]{1,0:T(8,128)} %get-tuple-element.13.stats_in), custom_call_target="tpu_custom_call" | custom-call | tf_op jit(solution)/shard_map/finish/pallas_call | solution.py:766
